TPU v7x, 32 devices: a whole 2x2x4 slice. The times are simulated.
32 devices in a mesh: req: 4 (over z), cp: 8 (over y, x, core).
Axes of the slice: x: 2, y: 2, z: 4, core: 2. Of those that a mesh axis runs over, the one named last changes fastest.
Arguments:
- hidden: bfloat16 [4, 256, 8192], P('req', 'cp'), may hold values from -8 to 8
- residual: bfloat16 [4, 256, 8192], P('req', 'cp'), may hold values from -6 to 6
- w_query: bfloat16 [8192, 8192], P(None, 'cp'), may hold values from -0.0625 to 0.0625
- w_keyval: bfloat16 [8192, 2048], P('cp'), may hold values from -0.0625 to 0.0625
- w_out: bfloat16 [8192, 8192], P('cp'), may hold values from -0.375 to 0.375
- kv_pool: bfloat16 [96, 128, 2048], P('req', 'cp'), may hold values from -6 to 6
- prefix_len: int32 [4], replicated, may hold values from 1 to 3072, as said below
- hit_holder: int32 [4, 24], replicated, may hold values from 0 to 3, as said below
- hit_slot: int32 [4, 24], replicated, may hold values from 0 to 23, as said below
- owner: int32 [4, 2], replicated, may hold values from 0 to 3, as said below
Outputs:
- layer_out: bfloat16 [4, 256, 8192], P('req', 'cp')
- new_cache: bfloat16 [4, 4, 128, 2048], P('req', None, 'cp')
Inputs may be any that keep to these rules, and one draw needn't show every extreme that they name: `hit_holder`: no holder holds more than 12 of one request's hits, and for every request one holder holds exactly 12. `hit_slot`: the hits of one request name distinct slots. `prefix_len`: some request has the longest prefix and some the shortest. No owner receives more than 1 new blocks of one request, and every request sends exactly 1 to one owner.
All inputs are finite; a program needn't handle non-finite values.
Results may differ from a plain program's by a relative error of at most 0.013.
Values may be sent and summed in bfloat16 or wider, within the bound.
No kernel may reach another device: no remote copies, remote signals or barrier semaphores. Data moves between devices by JAX's collectives and lax.ppermute only.
A program may use at most 192 MiB of HBM per device.

v0:
```python
import math

import jax
import jax.numpy as jnp
from jax import lax
from jax.sharding import PartitionSpec as P

KVH = 8
HD = 128
BLK = 128


def frequencies(width):
    half_width = width // 2
    base_freq = jnp.power(
        jnp.float32(500000.0), -jnp.arange(half_width, dtype=jnp.float32) * (2.0 / width)
    )
    wavelength = 2.0 * math.pi / base_freq
    blended = (8192.0 / wavelength - 1.0) / 3.0
    middle = (1.0 - blended) * base_freq / 8.0 + blended * base_freq
    return jnp.where(
        wavelength < 2048.0, base_freq, jnp.where(wavelength > 8192.0, base_freq / 8.0, middle)
    )


def rotate(values, positions):
    half_width = values.shape[-1] // 2
    inverse = frequencies(values.shape[-1])
    angles = positions.astype(jnp.float32)[:, None] * inverse[None, :]
    cosine = jnp.cos(angles)[:, None, :]
    sine_table = jnp.sin(angles)[:, None, :]
    first_half = values[..., :half_width]
    second = values[..., half_width:]
    return jnp.concatenate(
        [first_half * cosine - second * sine_table, second * cosine + first_half * sine_table],
        axis=-1,
    )


def fresh_keyvals(summed, positions):
    row_count = summed.shape[0]
    key_width = KVH * HD
    rotated = rotate(summed[:, :key_width].reshape(row_count, KVH, HD), positions).reshape(
        row_count, key_width
    )
    return jnp.concatenate([rotated, summed[:, key_width:]], axis=1).astype(jnp.bfloat16)


def local(
    hidden, residual, w_query, w_keyval, w_out, kv_pool, prefix_len, hit_holder, hit_slot, owner
):
    cp_count = lax.axis_size("cp")
    group_id = lax.axis_index("req")
    cp_rank = lax.axis_index("cp")
    tok_rows = hidden.shape[1]
    stretch_rows = tok_rows * cp_count
    head_count = w_query.shape[1] // HD
    slice_rows = w_keyval.shape[0]
    kv_width = w_keyval.shape[1] // 2
    block_rows = kv_pool.shape[1]
    request_count = hit_holder.shape[0]
    prefix_blocks = hit_holder.shape[1]
    span = prefix_blocks * BLK
    new_blocks = owner.shape[1]
    owner_cap = (new_blocks + 1) // 2
    holder_cap = prefix_blocks // 2
    heads_share = cp_count // KVH
    kv_head = cp_rank // heads_share
    score_scale = HD ** (-0.5)
    length = prefix_len[group_id]
    positions = length + jnp.arange(stretch_rows, dtype=jnp.int32)
    gathered = lax.all_gather(hidden[0], "cp", axis=0, tiled=True)
    queries = rotate(
        jnp.dot(gathered, w_query, preferred_element_type=jnp.float32).reshape(
            stretch_rows, head_count, HD
        ),
        positions,
    ).astype(jnp.bfloat16)
    columns = lax.dynamic_slice_in_dim(gathered, cp_rank * slice_rows, slice_rows, 1)
    summed = lax.psum(jnp.dot(columns, w_keyval, preferred_element_type=jnp.float32), "cp")
    fresh_kv = fresh_keyvals(summed, positions)
    fresh_keys = lax.dynamic_slice_in_dim(fresh_kv, kv_head * HD, HD, 1)
    fresh_values = lax.dynamic_slice_in_dim(fresh_kv, kv_width + kv_head * HD, HD, 1)
    blocks = fresh_kv.reshape(new_blocks, BLK, 2 * kv_width)
    my_rows = lax.dynamic_slice_in_dim(blocks, cp_rank * block_rows, block_rows, 1)
    slot_ids = jnp.arange(holder_cap, dtype=jnp.int32)
    holds_hit = hit_holder == group_id
    hit_order = jnp.cumsum(holds_hit.astype(jnp.int32), axis=1) - 1
    picked = holds_hit[:, None, :] & (hit_order[:, None, :] == slot_ids[None, :, None])
    sources = jnp.sum(jnp.where(picked, hit_slot[:, None, :], 0), axis=2)
    filled = jnp.any(picked, axis=2)
    outgoing = jnp.where(filled[:, :, None, None], kv_pool[sources], jnp.zeros((), jnp.bfloat16))
    arrived = lax.all_to_all(outgoing, "req", split_axis=0, concat_axis=0, tiled=True)
    my_holders = hit_holder[group_id]
    hit_index = jnp.arange(prefix_blocks, dtype=jnp.int32)
    earlier = (my_holders[:, None] == my_holders[None, :]) & (
        hit_index[:, None] > hit_index[None, :]
    )
    hit_rank = jnp.sum(earlier.astype(jnp.int32), axis=1)
    prefix_rows = arrived.reshape(request_count * holder_cap, block_rows, 2 * kv_width)[
        my_holders * holder_cap + hit_rank
    ]
    whole_blocks = lax.all_gather(prefix_rows, "cp", axis=1, tiled=True).reshape(span, 2 * kv_width)
    prefix_keys = lax.dynamic_slice_in_dim(whole_blocks, kv_head * HD, HD, 1)
    prefix_values = lax.dynamic_slice_in_dim(whole_blocks, kv_width + kv_head * HD, HD, 1)
    all_keys = jnp.concatenate([prefix_keys, fresh_keys], axis=0)
    all_values = jnp.concatenate([prefix_values, fresh_values], axis=0)
    key_index = jnp.arange(span + stretch_rows, dtype=jnp.int32)[None, :]
    query_index = jnp.arange(stretch_rows, dtype=jnp.int32)[:, None]
    visible = jnp.where(key_index < span, key_index < length, key_index - span <= query_index)
    scores = (
        jnp.einsum("qhd,kd->hqk", queries, all_keys, preferred_element_type=jnp.float32)
        * score_scale
    )
    scores = jnp.where(visible[None, :, :], scores, -1e30)
    row_peak = jnp.max(scores, axis=2, keepdims=True)
    weights = jnp.exp(scores - row_peak)
    denominator = jnp.sum(weights, axis=2, keepdims=True)
    mixed_heads = jnp.einsum(
        "hqk,kd->qhd", weights.astype(jnp.bfloat16), all_values, preferred_element_type=jnp.float32
    )
    mixed_heads = mixed_heads / jnp.transpose(denominator, (1, 0, 2))
    attended = mixed_heads.astype(jnp.bfloat16).reshape(stretch_rows, head_count * HD)
    projected = lax.psum_scatter(
        jnp.dot(attended, w_out, preferred_element_type=jnp.float32).astype(jnp.bfloat16),
        "cp",
        scatter_dimension=0,
        tiled=True,
    ).astype(jnp.float32)
    layer_out = (residual[0].astype(jnp.float32) + projected).astype(jnp.bfloat16)[None]
    my_owners = owner[group_id]
    block_ids = jnp.arange(new_blocks, dtype=jnp.int32)
    before = (my_owners[:, None] == my_owners[None, :]) & (block_ids[:, None] > block_ids[None, :])
    owner_rank = jnp.sum(before.astype(jnp.int32), axis=1)
    targets = jnp.arange(request_count, dtype=jnp.int32)[:, None, None]
    cap_ids = jnp.arange(owner_cap, dtype=jnp.int32)[None, :, None]
    chosen = (my_owners[None, None, :] == targets) & (owner_rank[None, None, :] == cap_ids)
    block_pick = jnp.sum(jnp.where(chosen, block_ids[None, None, :], 0), axis=2)
    present = jnp.any(chosen, axis=2)
    sending = jnp.where(present[:, :, None, None], my_rows[block_pick], jnp.zeros((), jnp.bfloat16))
    landed = lax.all_to_all(sending, "req", split_axis=0, concat_axis=0, tiled=True)
    new_cache = landed.reshape(1, request_count * owner_cap, block_rows, 2 * kv_width)
    return (layer_out, new_cache)


def solution(mesh):
    in_specs = (
        P("req", "cp", None),
        P("req", "cp", None),
        P(None, "cp"),
        P("cp", None),
        P("cp", None),
        P("req", "cp", None),
        P(),
        P(),
        P(),
        P(),
    )
    out_specs = (P("req", "cp", None), P("req", None, "cp", None))
    return jax.shard_map(local, mesh=mesh, in_specs=in_specs, out_specs=out_specs, check_vma=False)
```

profile of v0, /device:TPU:0, one launch (start us, length us, event | category | flops | bytes accessed | tf_op | source)
XLA Modules:
  0.0 301.5 jit_solution(18385334535465333647)
XLA Ops:
  7.2 0.7 all-gather.7.cloned.1.call-update
  7.9 0.7 fusion.48
  8.6 0.2 reduce_window_sum.11
  8.8 0.3 fusion.35
  9.1 0.1 copy.36
  9.2 1.0 select_reduce_fusion
  10.4 2.5 gather_fusion
  12.9 3.9 %broadcast_select_fusion = bf16[4,12,16,2048]{3,2,1,0:T(8,128)(2,1)} fusion(bf16[4,12,16,2048]{3,2,1,0:T(8,128)(2,1)} %bitcast.89, pred[4,12]{1,0:T(4,128)(4,1)S(1)} %copy.36), kind=kLoop, calls=%fused_computation.15 | loop fusion | flops 1572864 | bytes 6291504 | tf_op jit(solution)/shard_map/jit(_where)/select_n | solution.py:92
  16.8 6.3 %all-to-all-start = ((bf16[4,12,16,2048]{3,2,1,0:T(8,128)(2,1)}), bf16[4,12,16,2048]{3,2,1,0:T(8,128)(2,1)}, u32[]{:S(2)}, u32[]{:S(2)}) async-start(bf16[4,12,16,2048]{3,2,1,0:T(8,128)(2,1)} %broadcast_select_fusion), calls=%async_computation | async-start | bytes 6291456 | tf_op jit(solution)/shard_map/all_to_all | solution.py:93
  23.1 26.3 %all-gather.7.cloned.1.call-done = bf16[1,256,8192]{2,1,0:T(8,128)(2,1)} async-done(((bf16[1,32,8192]{2,1,0:T(8,128)(2,1)}), bf16[1,256,8192]{2,1,0:T(8,128)(2,1)}) %all-gather.7.cloned.1.call-update) | async-done | bytes 4194320 | tf_op jit(solution)/shard_map/all_gather | solution.py:72
  49.4 4.9 %fusion.27 = f32[256,2048]{1,0:T(8,128)} fusion(bf16[1024,2048]{1,0:T(8,128)(2,1)} %param.13, bf16[1,256,8192]{2,1,0:T(8,128)(2,1)} %all-gather.7.cloned.1.call-done, s32[]{:T(128)S(6)} %select_n.121), kind=kOutput, calls=%fused_computation.46 | convolution fusion | flops 1073741824 | bytes 6815748 | tf_op jit(solution)/shard_map/dot_general | solution.py:80
  54.4 0.2 convert_reduce_fusion
  54.6 39.3 %all-to-all-done = bf16[4,12,16,2048]{3,2,1,0:T(8,128)(2,1)} async-done(((bf16[4,12,16,2048]{3,2,1,0:T(8,128)(2,1)}), bf16[4,12,16,2048]{3,2,1,0:T(8,128)(2,1)}, u32[]{:S(2)}, u32[]{:S(2)}) %all-to-all-start) | async-done | bytes 3145760 | tf_op jit(solution)/shard_map/all_to_all | solution.py:93
  93.9 3.8 %gather_fusion.1 = bf16[24,16,2048]{2,1,0:T(8,128)(2,1)} fusion(bf16[48,16,2048]{2,1,0:T(8,128)(2,1)} %bitcast.3, s32[1024]{0:T(1024)S(1)} %pad_clamp_fusion.1), kind=kCustom, calls=%fused_computation.1 | custom fusion | bytes 3145824 | tf_op jit(solution)/shard_map/gather | solution.py:100
  97.7 0.2 reduce-scatter.2.cloned.1.call-start
  97.9 0.6 dynamic_slice.32
  98.5 0.7 add_convert_fusion.1
  99.2 0.7 iota_compare_fusion.2
  99.9 0.5 multiply_cosine_fusion
  100.4 4.4 %fusion.8 = pred[256,3328]{0,1:T(8,128)(4,1)} fusion(s32[3328]{0:T(1024)S(1)} %iota_add_fusion, pred[3328]{0:T(1024)(128)(4,1)S(1)} %get-tuple-element.20, pred[3328]{0:T(1024)(128)(4,1)S(1)} %get-tuple-element.21), kind=kLoop, calls=%fused_computation.14 | loop fusion | flops 1703936 | bytes 871936 | tf_op jit(solution)/shard_map/jit(_where)/select_n | solution.py:110
  104.8 9.6 %fusion.9 = f32[32,8,8,128]{3,1,2,0:T(8,128)S(1)} fusion(bf16[8192,1024]{1,0:T(8,128)(2,1)} %param.12, bf16[1,256,8192]{2,1,0:T(8,128)(2,1)} %all-gather.7.cloned.1.call-done), kind=kOutput, calls=%fused_computation.16 | convolution fusion | flops 4294967296 | bytes 22020096 | tf_op jit(solution)/shard_map/dot_general | solution.py:74
  114.4 0.2 copy.58
  114.6 0.3 fusion.49
  114.9 1.4 subtract_convert_fusion
  116.4 1.3 slice_bitcast_fusion
  117.7 0.2 copy.57
  117.9 1.3 slice.38
  119.2 0.3 fusion.50
  119.5 0.4 multiply_subtract_fusion
  120.0 0.3 copy_bitcast_fusion
  120.2 0.1 fusion.33
  120.3 68.8 %all-gather.5.cloned.1.call-done = bf16[24,128,2048]{2,1,0:T(8,128)(2,1)} async-done(((bf16[24,16,2048]{2,1,0:T(8,128)(2,1)}), bf16[24,128,2048]{2,1,0:T(8,128)(2,1)}) %all-gather.5.cloned.1.call-update) | async-done | bytes 12582928 | tf_op jit(solution)/shard_map/all_gather | solution.py:103
  189.1 1.5 constant_dynamic-slice_fusion.2
  190.7 12.9 %fusion.2 = (f32[8,256]{1,0:T(8,128)S(1)}, f32[3328,256,8]{1,0,2:T(8,128)}) fusion(pred[256,3328]{0,1:T(8,128)(4,1)S(1)} %copy-done.2, bf16[256,8,64]{2,0,1:T(8,128)(2,1)} %get-tuple-element.7, bf16[256,8,64]{2,0,1:T(8,128)(2,1)} %get-tuple-element.6, bf16[256,128]{1,0:T(8,128)(2,1)S(1)} %get-tuple-element.11, bf16[3072,128]{1,0:T(8,128)(2,1)S(1)} %get-tuple-element.5), kind=kOutput, calls=%fused_computation.7 | convolution fusion | flops 1768028160 | bytes 29499392 | tf_op jit(solution)/shard_map/qhd,kd->hqk/dot_general | solution.py:112
  203.6 12.1 %fusion = f32[8,256]{1,0:T(8,128)S(1)} fusion(f32[3328,256,8]{1,0,2:T(8,128)} %get-tuple-element.19, f32[8,256]{1,0:T(8,128)S(1)} %get-tuple-element.18, pred[256,3328]{0,1:T(8,128)(4,1)S(1)} %copy-done.2), kind=kLoop, calls=%fused_computation.5 | loop fusion | flops 27260928 | bytes 28131328 | tf_op jit(solution)/shard_map/reduce_sum | solution.py:118
  215.7 12.7 %divide_convert_fusion = bf16[256,8,128]{0,2,1:T(8,128)(2,1)S(1)} fusion(f32[3328,256,8]{1,0,2:T(8,128)} %get-tuple-element.19, f32[8,256]{1,0:T(8,128)S(1)} %get-tuple-element.18, pred[256,3328]{0,1:T(8,128)(4,1)S(1)} %copy-done.2, bf16[256,128]{1,0:T(8,128)(2,1)S(1)} %get-tuple-element.10, bf16[3072,128]{1,0:T(8,128)(2,1)S(1)} %get-tuple-element.4, ...), kind=kOutput, calls=%fused_computation.29 | convolution fusion | flops 1774321664 | bytes 29507584 | tf_op jit(solution)/shard_map/hqk,kd->qhd/dot_general | solution.py:119
  228.4 12.3 %convolution_convert_fusion = bf16[256,8192]{1,0:T(8,128)(2,1)} fusion(bf16[256,1024]{0,1:T(8,128)(2,1)S(1)} %bitcast.94, bf16[1024,8192]{1,0:T(8,128)(2,1)} %param.14), kind=kOutput, calls=%fused_computation.10 | convolution fusion | flops 4297064448 | bytes 21495808 | tf_op jit(solution)/shard_map/dot_general | solution.py:125
  240.7 0.7 copy-done.4
  241.3 0.2 fusion.39
  241.5 0.2 fusion.38
  241.9 0.3 maximum_convert_fusion
  242.2 0.3 copy.40
  242.6 0.2 concatenate.30
  242.8 0.6 gather_fusion.2
  243.5 13.7 %all_to_all.10 = bf16[4,1,16,2048]{3,2,1,0:T(8,128)(2,1)S(1)} all-to-all(bf16[4,1,16,2048]{3,2,1,0:T(8,128)(2,1)S(1)} %fusion.30), channel_id=1, replica_groups=mesh['req'=4,'cp'=8] {'req'}, dimensions={0} | all-to-all | bytes 524288 | tf_op jit(solution)/shard_map/all_to_all | solution.py:141
  257.2 35.0 %reduce-scatter.2.cloned.1.call-done = bf16[32,8192]{1,0:T(8,128)(2,1)} async-done(((bf16[256,8192]{1,0:T(8,128)(2,1)}), bf16[32,8192]{1,0:T(8,128)(2,1)}) %reduce-scatter.2.cloned.1.call-update) | async-done | bytes 524304 | tf_op jit(solution)/shard_map/reduce_scatter | solution.py:124
  292.2 2.1 fusion.23
  294.3 0.7 copy.70
  (35 shorter events, 0.7 us)
Async XLA Ops:
  7.2 3.2 %copy-start = (bf16[24,16,2048]{2,1,0:T(8,128)(2,1)S(1)}, bf16[24,16,2048]{2,1,0:T(8,128)(2,1)}, u32[]{:S(2)}) copy-start(bf16[24,16,2048]{2,1,0:T(8,128)(2,1)} %param.15) | copy-start | bytes 4718596
  7.2 42.2 %all-gather.7.cloned.1.call-start = ((), (), s32[]{:S(2)}) async-start(), calls=%async_computation.6 | async-start | bytes 4718592 | tf_op jit(solution)/shard_map/all_gather | solution.py:72
  16.8 77.1 %all-to-all-start = ((bf16[4,12,16,2048]{3,2,1,0:T(8,128)(2,1)}), bf16[4,12,16,2048]{3,2,1,0:T(8,128)(2,1)}, u32[]{:S(2)}, u32[]{:S(2)}) async-start(bf16[4,12,16,2048]{3,2,1,0:T(8,128)(2,1)} %broadcast_select_fusion), calls=%async_computation | async-start | bytes 6291456 | tf_op jit(solution)/shard_map/all_to_all | solution.py:93
  23.1 93.3 %all-reduce.2.cloned.1.call-start = ((), (), s32[]{:S(2)}) async-start(), calls=%async_computation.3 | async-start | bytes 4194304 | tf_op jit(solution)/shard_map/psum | solution.py:80
  23.1 31.2 %copy-start.3 = (s32[4,24]{1,0:T(4,128)S(1)}, s32[4,24]{1,0:T(4,128)}, u32[]{:S(2)}) copy-start(s32[4,24]{1,0:T(4,128)} %param.17) | copy-start | bytes 1156
  54.3 43.7 %copy-start.5 = (s32[4]{0:T(128)S(1)}, s32[4]{0:T(128)}, u32[]{:S(2)}) copy-start(s32[4]{0:T(128)} %param.16) | copy-start | bytes 52
  54.3 134.9 %all-gather.5.cloned.1.call-start = ((), (), s32[]{:S(2)}) async-start(), calls=%async_computation.5 | async-start | bytes 14155776 | tf_op jit(solution)/shard_map/all_gather | solution.py:103
  97.7 194.5 %reduce-scatter.2.cloned.1.call-start = ((), (), s32[]{:S(2)}) async-start(), calls=%async_computation.4 | async-start | bytes 4718592 | tf_op jit(solution)/shard_map/reduce_scatter | solution.py:124
  119.5 71.1 %copy-start.2 = (pred[256,3328]{0,1:T(8,128)(4,1)S(1)}, pred[256,3328]{0,1:T(8,128)(4,1)}, u32[]{:S(2)}) copy-start(pred[256,3328]{0,1:T(8,128)(4,1)} %fusion.8) | copy-start | bytes 2555908
  240.7 0.7 copy-start.4
  241.8 53.2 %copy-start.1 = (bf16[24,16,2048]{2,1,0:T(8,128)(2,1)S(1)}, bf16[24,16,2048]{2,1,0:T(8,128)(2,1)}, u32[]{:S(2)}) copy-start(bf16[24,16,2048]{2,1,0:T(8,128)(2,1)} %param.15) | copy-start | bytes 4718596
Sparse Core Ops, SparseCore 0:
  9.9 39.4 all-gather.6
  54.4 61.5 all-reduce.1
  118.0 71.1 all-gather.4
  240.8 51.3 reduce-scatter.1
where the time goes:
time: 302 us
  waiting for transfers between devices  170 us (56%)
  matrix products  52.4 us (17%)
  other arithmetic  29.7 us (10%)
  local copies, waits for them, and re-layouts  15.1 us (5%)
  between operations  14 us (5%)
  blocking collectives  13.7 us (5%)
  starting transfers between devices  6.62 us (2%)
    all_gather x1, waiting for transfers between devices, local(): lax.all_gather(prefix_rows, 'cp', axis=1, tiled=True)  68.8 us
    all_to_all x1, waiting for transfers between devices, local(): lax.all_to_all(outgoing, 'req', split_axis=0, concat_axis=0, tiled=True)  39.3 us
    reduce_scatter x1, waiting for transfers between devices, local(): lax.psum_scatter(jnp.dot(attended, w_out, preferred_element_type=jnp.floa...  35 us
    all_gather x1, waiting for transfers between devices, local(): gathered = lax.all_gather(hidden[0], 'cp', axis=0, tiled=True)  26.3 us
    all_to_all x1, blocking collectives, local(): lax.all_to_all(sending, 'req', split_axis=0, concat_axis=0, tiled=True)  13.7 us
    dot_general x1, matrix products, local(): jnp.einsum('qhd,kd->hqk', queries, all_keys, preferred_element_type=jnp.f...  12.9 us
    dot_general x1, matrix products, local(): jnp.einsum('hqk,kd->qhd', weights.astype(jnp.bfloat16), all_values, prefe...  12.7 us
    dot_general x1, matrix products, local(): jnp.dot(attended, w_out, preferred_element_type=jnp.float32)  12.3 us
  transfers between devices with their start and end apart: 5, of which 4 were waited for; matrix products, arithmetic and copies ran while one was open for 14% of the time, Pallas kernels for 0%

commit v1 on v0

v1 whole, which is shorter than its diff:
```python
import functools
import math

import jax
import jax.numpy as jnp
from jax import lax
from jax.experimental import pallas as pl
from jax.experimental.pallas import tpu as pltpu
from jax.sharding import PartitionSpec as P

KVH = 8
HD = 128
BLK = 128
LOG2E = 1.4426950408889634


def frequencies(width):
    half_width = width // 2
    base_freq = jnp.power(
        jnp.float32(500000.0), -jnp.arange(half_width, dtype=jnp.float32) * (2.0 / width)
    )
    wavelength = 2.0 * math.pi / base_freq
    blended = (8192.0 / wavelength - 1.0) / 3.0
    middle = (1.0 - blended) * base_freq / 8.0 + blended * base_freq
    return jnp.where(
        wavelength < 2048.0, base_freq, jnp.where(wavelength > 8192.0, base_freq / 8.0, middle)
    )


def rope_tables(positions):
    angles = positions.astype(jnp.float32)[:, None] * frequencies(HD)[None, :]
    cosine, sine = jnp.cos(angles), jnp.sin(angles)
    return jnp.concatenate([cosine, cosine], axis=1), jnp.concatenate([-sine, sine], axis=1)


def attention_kernel(tile, chunk, stretch, length_ref, q_ref, cos_ref, sin_ref, kv_ref, fresh_ref, out_ref):
    length = length_ref[0]
    row0 = pl.program_id(1) * tile
    raw = q_ref[...]
    query = (raw * cos_ref[...] + pltpu.roll(raw, HD // 2, 1) * sin_ref[...]).astype(jnp.bfloat16)
    factor = HD ** (-0.5) * LOG2E

    def scores(keys):
        return lax.dot_general(
            query, keys, (((1,), (1,)), ((), ())), preferred_element_type=jnp.float32
        )

    def update(carry, part, values):
        peak, total, mixed = carry
        new_peak = jnp.maximum(peak, jnp.max(part, axis=1, keepdims=True))
        weights = jnp.exp2((part - new_peak) * factor)
        shrink = jnp.exp2((peak - new_peak) * factor)
        total = total * shrink + jnp.sum(weights, axis=1, keepdims=True)
        mixed = mixed * shrink + jnp.dot(
            weights.astype(jnp.bfloat16), values, preferred_element_type=jnp.float32
        )
        return new_peak, total, mixed

    carry = (
        jnp.full((tile, 1), -1e30, jnp.float32),
        jnp.zeros((tile, 1), jnp.float32),
        jnp.zeros((tile, HD), jnp.float32),
    )
    part = scores(fresh_ref[:, :HD])
    columns = lax.broadcasted_iota(jnp.int32, part.shape, 1)
    rows = lax.broadcasted_iota(jnp.int32, part.shape, 0) + row0
    carry = update(carry, jnp.where(columns <= rows, part, -1e30), fresh_ref[:, HD:])

    def whole(step, carry):
        at = pl.multiple_of(step * chunk, chunk)
        return update(carry, scores(kv_ref[pl.ds(at, chunk), :HD]), kv_ref[pl.ds(at, chunk), HD:])

    full = length // chunk
    carry = lax.fori_loop(0, full, whole, carry)

    def rest(step, carry):
        at = pl.multiple_of(step * chunk, chunk)
        part = scores(kv_ref[pl.ds(at, chunk), :HD])
        seen = lax.broadcasted_iota(jnp.int32, part.shape, 1) + at < length
        return update(carry, jnp.where(seen, part, -1e30), kv_ref[pl.ds(at, chunk), HD:])

    last = (length + chunk - 1) // chunk
    peak, total, mixed = lax.fori_loop(full, last, rest, carry)
    out_ref[...] = (mixed / total).astype(jnp.bfloat16)


def attention(length, raw_queries, cosine, sine, prefix, fresh):
    rows, width = raw_queries.shape
    tile = min(256, rows)
    chunk = 512
    return pl.pallas_call(
        functools.partial(attention_kernel, tile, chunk, rows),
        grid_spec=pltpu.PrefetchScalarGridSpec(
            num_scalar_prefetch=1,
            grid=(width // HD, rows // tile),
            in_specs=[
                pl.BlockSpec((tile, HD), lambda h, t, n: (t, h)),
                pl.BlockSpec((tile, HD), lambda h, t, n: (t, 0)),
                pl.BlockSpec((tile, HD), lambda h, t, n: (t, 0)),
                pl.BlockSpec(prefix.shape, lambda h, t, n: (0, 0)),
                pl.BlockSpec(fresh.shape, lambda h, t, n: (0, 0)),
            ],
            out_specs=pl.BlockSpec((tile, HD), lambda h, t, n: (t, h)),
        ),
        out_shape=jax.ShapeDtypeStruct((rows, width), jnp.bfloat16),
        compiler_params=pltpu.CompilerParams(vmem_limit_bytes=24 * 1024 * 1024),
        cost_estimate=pl.CostEstimate(
            flops=4 * rows * width * (prefix.shape[0] + rows),
            bytes_accessed=rows * width * 6,
            transcendentals=rows * width // HD * (prefix.shape[0] + rows),
        ),
    )(length.reshape(1), raw_queries, cosine, sine, prefix, fresh)


def swap(array, bit, count):
    return lax.ppermute(array, "cp", [(i, i ^ bit) for i in range(count)])


def pick(array, index, axis):
    return lax.dynamic_index_in_dim(array, index, axis, keepdims=False)


def add(one, two):
    return one.astype(jnp.float32) + two.astype(jnp.float32)


def scatter_sum(part, rank):
    rows, width = part.shape
    core, x, y = rank % 2, rank // 2 % 2, rank // 4
    view = part.reshape(2, 2, 2, rows // 8, width)
    got = swap(pick(view, 1 - core, 2), 1, 8)
    pair = add(pick(view, core, 2), got).astype(jnp.bfloat16)
    half = width // 2
    one, two = pair[..., :half], pair[..., half:]
    got_one = swap(pick(one, 1 - x, 1), 2, 8)
    got_two = swap(pick(two, 1 - y, 0), 4, 8)
    one = add(pick(one, x, 1), got_one)
    two = add(pick(two, y, 0), got_two)
    end_one = swap(pick(one, 1 - y, 0).astype(jnp.bfloat16), 4, 8)
    end_two = swap(pick(two, 1 - x, 0).astype(jnp.bfloat16), 2, 8)
    one = add(pick(one, y, 0), end_one)
    two = add(pick(two, x, 0), end_two)
    return jnp.concatenate([one, two], axis=1)


def local(
    hidden, residual, w_query, w_keyval, w_out, kv_pool, prefix_len, hit_holder, hit_slot, owner
):
    cp_count = lax.axis_size("cp")
    group_id = lax.axis_index("req")
    cp_rank = lax.axis_index("cp")
    tok_rows = hidden.shape[1]
    stretch_rows = tok_rows * cp_count
    slice_rows = w_keyval.shape[0]
    block_rows = kv_pool.shape[1]
    request_count = hit_holder.shape[0]
    prefix_blocks = hit_holder.shape[1]
    new_blocks = owner.shape[1]
    owner_cap = (new_blocks + 1) // 2
    holder_cap = prefix_blocks // 2
    heads_share = cp_count // KVH
    length = prefix_len[group_id]
    positions = length + jnp.arange(stretch_rows, dtype=jnp.int32)
    cosine, sine = rope_tables(positions)

    slot_ids = jnp.arange(holder_cap, dtype=jnp.int32)
    holds_hit = hit_holder == group_id
    hit_order = jnp.cumsum(holds_hit.astype(jnp.int32), axis=1) - 1
    picked = holds_hit[:, None, :] & (hit_order[:, None, :] == slot_ids[None, :, None])
    sources = jnp.sum(jnp.where(picked, hit_slot[:, None, :], 0), axis=2)
    by_head = kv_pool.reshape(-1, block_rows, 2, KVH, HD)[sources]
    by_head = jnp.transpose(by_head, (0, 4, 1, 2, 3, 5))
    by_head = jnp.repeat(by_head, heads_share, axis=1)
    sending = by_head.reshape(
        request_count * cp_count, holder_cap * block_rows, 2 * HD
    )
    arrived = lax.all_to_all(sending, ("req", "cp"), split_axis=0, concat_axis=0, tiled=True)

    gathered = lax.all_gather(hidden[0], "cp", axis=0, tiled=True)
    raw_queries = jnp.dot(gathered, w_query, preferred_element_type=jnp.float32)
    columns = lax.dynamic_slice_in_dim(gathered, cp_rank * slice_rows, slice_rows, 1)
    partial_kv = jnp.dot(columns, w_keyval, preferred_element_type=jnp.float32)
    partial_kv = jnp.transpose(
        partial_kv.reshape(stretch_rows, 2, KVH, HD), (2, 0, 1, 3)
    ).reshape(KVH, stretch_rows, 2 * HD)
    partial_kv = jnp.repeat(partial_kv, heads_share, axis=0)
    summed = lax.psum_scatter(partial_kv, "cp", scatter_dimension=0, tiled=True)[0]
    keys = summed[:, :HD]
    keys = keys * cosine + jnp.roll(keys, HD // 2, axis=1) * sine
    fresh = jnp.concatenate([keys, summed[:, HD:]], axis=1).astype(jnp.bfloat16)

    my_holders = hit_holder[group_id]
    hit_index = jnp.arange(prefix_blocks, dtype=jnp.int32)
    earlier = (my_holders[:, None] == my_holders[None, :]) & (
        hit_index[:, None] > hit_index[None, :]
    )
    hit_rank = jnp.sum(earlier.astype(jnp.int32), axis=1)
    arrived = arrived.reshape(request_count, cp_count, holder_cap, block_rows, 2 * HD)
    prefix = arrived[my_holders, :, hit_rank].reshape(prefix_blocks * BLK, 2 * HD)

    attended = attention(length, raw_queries, cosine, sine, prefix, fresh)

    if cp_count == 8:
        wide = w_out.shape[1] // 2
        sums = [
            scatter_sum(
                jnp.dot(
                    attended, w_out[:, at : at + wide], preferred_element_type=jnp.float32
                ).astype(jnp.bfloat16),
                cp_rank,
            )
            for at in range(0, w_out.shape[1], wide)
        ]
        projected = jnp.concatenate(sums, axis=1)
    else:
        projected = lax.psum_scatter(
            jnp.dot(attended, w_out, preferred_element_type=jnp.float32).astype(jnp.bfloat16),
            "cp",
            scatter_dimension=0,
            tiled=True,
        ).astype(jnp.float32)
    layer_out = (residual[0].astype(jnp.float32) + projected).astype(jnp.bfloat16)[None]

    my_owners = owner[group_id]
    block_ids = jnp.arange(new_blocks, dtype=jnp.int32)
    before = (my_owners[:, None] == my_owners[None, :]) & (block_ids[:, None] > block_ids[None, :])
    owner_rank = jnp.sum(before.astype(jnp.int32), axis=1)
    targets = jnp.arange(request_count, dtype=jnp.int32)[:, None, None]
    cap_ids = jnp.arange(owner_cap, dtype=jnp.int32)[None, :, None]
    chosen = (my_owners[None, None, :] == targets) & (owner_rank[None, None, :] == cap_ids)
    block_pick = jnp.sum(jnp.where(chosen, block_ids[None, None, :], 0), axis=2)
    present = jnp.any(chosen, axis=2)
    blocks = fresh.reshape(new_blocks, cp_count, block_rows, 2 * HD)[block_pick]
    blocks = jnp.where(present[:, :, None, None, None], blocks, jnp.zeros((), jnp.bfloat16))
    blocks = jnp.transpose(blocks, (0, 2, 1, 3, 4)).reshape(
        request_count * cp_count, owner_cap * block_rows, 2 * HD
    )
    landed = lax.all_to_all(blocks, ("req", "cp"), split_axis=0, concat_axis=0, tiled=True)
    landed = landed.reshape(request_count, cp_count, owner_cap, block_rows, 2, HD)[:, ::heads_share]
    new_cache = jnp.transpose(landed, (0, 2, 3, 4, 1, 5)).reshape(
        1, request_count * owner_cap, block_rows, 2 * KVH * HD
    )
    return (layer_out, new_cache)


def solution(mesh):
    in_specs = (
        P("req", "cp", None),
        P("req", "cp", None),
        P(None, "cp"),
        P("cp", None),
        P("cp", None),
        P("req", "cp", None),
        P(),
        P(),
        P(),
        P(),
    )
    out_specs = (P("req", "cp", None), P("req", None, "cp", None))
    return jax.shard_map(local, mesh=mesh, in_specs=in_specs, out_specs=out_specs, check_vma=False)
```

time: 302 us -> 211 us (0.70)
  waiting for transfers between devices: 170 us -> 84.2 us
  starting transfers between devices: 6.62 us -> 39.1 us
  matrix products: 52.4 us -> 24.6 us
  other arithmetic: 29.7 us -> 8.79 us
  local copies, waits for them, and re-layouts: 15.1 us -> 29.7 us
  blocking collectives: 13.7 us -> 0 us
  Pallas kernels: 0 us -> 9.25 us
    all_gather x1 -> x0, waiting for transfers between devices: 68.8 us -> none  [local(): lax.all_gather(prefix_rows, 'cp', axis=1, tiled=True)]
    dot_general x5 -> x4, matrix products: 52.4 us -> 24.6 us  [the longest x2 11.5 us: local(): jnp.dot(attended, w_out[:, at:at + wide], preferred_element_type=jnp.floa...]
    reduce_scatter x1, waiting for transfers between devices: 35 us -> 8.44 us  [local(): lax.psum_scatter(partial_kv, 'cp', scatter_dimension=0, tiled=True)[0]]
    all_to_all x1 -> x2, starting transfers between devices: 6.32 us -> 30.6 us  [the longest x1 23.2 us: local(): lax.all_to_all(blocks, ('req', 'cp'), split_axis=0, concat_axis=0, tiled=...]
    all_to_all x1 -> x2, waiting for transfers between devices: 39.3 us -> 20.3 us  [the longest x1 15.8 us: local(): lax.all_to_all(sending, ('req', 'cp'), split_axis=0, concat_axis=0, tiled...]
    all_gather x1, waiting for transfers between devices: 26.3 us -> 44.6 us  [local(): gathered = lax.all_gather(hidden[0], 'cp', axis=0, tiled=True)]
    all_to_all x1 -> x0, blocking collectives: 13.7 us -> none  [local(): lax.all_to_all(sending, 'req', split_axis=0, concat_axis=0, tiled=True)]
    reduce_sum x1 -> x0, other arithmetic: 12.1 us -> none  [local(): denominator = jnp.sum(weights, axis=2, keepdims=True)]
  transfers between devices with their start and end apart: 5 -> 14, of which waited for: 4 -> 11; matrix products, arithmetic and copies ran while one was open for 14% -> 24% of each run, Pallas kernels for 0% -> 0%
where the time goes in v1:
time: 211 us; the launch traced here: 210 us
  waiting for transfers between devices  84.2 us (40%)
  starting transfers between devices  39.1 us (19%)
  local copies, waits for them, and re-layouts  29.7 us (14%)
  matrix products  24.6 us (12%)
  between operations  14.5 us (7%)
  Pallas kernels  9.25 us (4%)
  other arithmetic  8.79 us (4%)
    all_gather x1, waiting for transfers between devices, local(): gathered = lax.all_gather(hidden[0], 'cp', axis=0, tiled=True)  44.6 us
    all_to_all x1, starting transfers between devices, local(): lax.all_to_all(blocks, ('req', 'cp'), split_axis=0, concat_axis=0, tiled=...  23.2 us
    all_to_all x1, waiting for transfers between devices, local(): lax.all_to_all(sending, ('req', 'cp'), split_axis=0, concat_axis=0, tiled...  15.8 us
    dot_general x2, matrix products, local(): jnp.dot(attended, w_out[:, at:at + wide], preferred_element_type=jnp.floa...  11.5 us
    ppermute x10, waiting for transfers between devices, swap(): return lax.ppermute(array, 'cp', [(i, i ^ bit) for i in range(count)])  10.1 us
    dot_general x1, matrix products, local(): raw_queries = jnp.dot(gathered, w_query, preferred_element_type=jnp.float32)  9.49 us
    pallas_call x1, Pallas kernels, attention(): pl.pallas_call(functools.partial(attention_kernel, tile, chunk, rows), gr...  9.25 us
    reduce_scatter x1, waiting for transfers between devices, local(): lax.psum_scatter(partial_kv, 'cp', scatter_dimension=0, tiled=True)[0]  8.44 us
  transfers between devices with their start and end apart: 14, of which 11 were waited for; matrix products, arithmetic and copies ran while one was open for 24% of the time, Pallas kernels for 0%

profile of v1, /device:TPU:0, one launch (start us, length us, event | category | flops | bytes accessed | tf_op | source)
XLA Modules:
  0.0 210.0 jit_solution(6357823803927924872)
XLA Ops:
  7.2 0.7 all-gather.3.cloned.1.call-update
  7.9 1.8 copy.33
  10.5 2.7 %gather_fusion = bf16[48,16,2,8,128]{4,3,2,1,0:T(8,128)(2,1)} fusion(bf16[24,16,2,8,128]{4,3,2,1,0:T(8,128)(2,1)S(1)} %bitcast.128, s32[1024]{0:T(1024)S(1)} %pad_clamp_fusion.1), kind=kCustom, calls=%fused_computation | custom fusion | bytes 6291648 | tf_op jit(solution)/shard_map/gather | solution.py:171
  13.2 5.1 %copy.24 = bf16[4,8,12,16,2,128]{5,4,3,2,1,0:T(2,128)(2,1)S(1)} copy(bf16[4,8,12,16,2,128]{5,1,4,3,2,0:T(8,128)(2,1)} %bitcast.129) | data formatting | bytes 6291456 | tf_op jit(solution)/shard_map/transpose | solution.py:172
  18.3 3.8 %reshape_reshape_broadcast_in_dim.3 = bf16[32,192,256]{2,1,0:T(8,128)(2,1)} reshape(bf16[4,8,12,16,2,128]{5,4,3,2,1,0:T(2,128)(2,1)S(1)} %copy.24) | data formatting | bytes 6291456 | tf_op jit(solution)/shard_map/reshape;reshape;broadcast_in_dim | solution.py:174
  22.2 7.4 %all-to-all-start = ((bf16[32,192,256]{2,1,0:T(8,128)(2,1)}), bf16[32,192,256]{2,1,0:T(8,128)(2,1)}, u32[]{:S(2)}, u32[]{:S(2)}) async-start(bf16[32,192,256]{2,1,0:T(8,128)(2,1)} %reshape_reshape_broadcast_in_dim.3), calls=%async_computation | async-start | bytes 6291456 | tf_op jit(solution)/shard_map/all_to_all | solution.py:177
  30.0 44.6 %all-gather.3.cloned.1.call-done = bf16[1,256,8192]{2,1,0:T(8,128)(2,1)} async-done(((bf16[1,32,8192]{2,1,0:T(8,128)(2,1)}), bf16[1,256,8192]{2,1,0:T(8,128)(2,1)}) %all-gather.3.cloned.1.call-update) | async-done | bytes 4194320 | tf_op jit(solution)/shard_map/all_gather | solution.py:179
  74.6 3.6 %convolution_bitcast_fusion = f32[32,8,16,128]{3,1,2,0:T(8,128)S(1)} fusion(bf16[1024,2048]{1,0:T(8,128)(2,1)} %param.13, bf16[1,256,8192]{2,1,0:T(8,128)(2,1)} %all-gather.3.cloned.1.call-done, s32[]{:T(128)S(6)} %select_n.155), kind=kOutput, calls=%fused_computation.16 | convolution fusion | flops 1073741824 | bytes 6815748 | tf_op jit(solution)/shard_map/dot_general | solution.py:182
  78.2 0.4 copy.34
  78.6 1.1 copy.36
  79.7 2.7 %reshape_broadcast_in_dim_reshape.3 = f32[8,256,256]{2,1,0:T(8,128)} reshape(f32[8,256,2,128]{3,2,1,0:T(2,128)S(1)} %bitcast.131) | data formatting | bytes 4194304 | tf_op jit(solution)/shard_map/reshape;broadcast_in_dim;reshape | solution.py:186
  82.7 0.6 dynamic_slice.78.length_ref
  83.6 0.7 add_convert_fusion
  84.6 0.5 fusion.27
  85.1 15.8 %all-to-all-done = bf16[32,192,256]{2,1,0:T(8,128)(2,1)} async-done(((bf16[32,192,256]{2,1,0:T(8,128)(2,1)}), bf16[32,192,256]{2,1,0:T(8,128)(2,1)}, u32[]{:S(2)}, u32[]{:S(2)}) %all-to-all-start) | async-done | bytes 3145760 | tf_op jit(solution)/shard_map/all_to_all | solution.py:177
  100.9 2.7 %gather_fusion.1 = bf16[24,8,16,256]{3,2,1,0:T(8,128)(2,1)S(1)} fusion(bf16[4,8,12,16,256]{4,3,2,1,0:T(8,128)(2,1)} %bitcast.5, s32[24]{0:T(128)S(1)} %fusion.40), kind=kCustom, calls=%fused_computation.1 | custom fusion | bytes 3145920 | tf_op jit(solution)/shard_map/gather | solution.py:199
  103.7 9.5 %fusion.10.q_ref = f32[256,1024]{1,0:T(8,128)S(1)} fusion(bf16[8192,1024]{1,0:T(8,128)(2,1)} %param.12, bf16[1,256,8192]{2,1,0:T(8,128)(2,1)} %all-gather.3.cloned.1.call-done), kind=kOutput, calls=%fused_computation.9 | convolution fusion | flops 4294967296 | bytes 22020096 | tf_op jit(solution)/shard_map/dot_general | solution.py:180
  113.2 8.4 %reduce-scatter.2.cloned.1.call-done = f32[1,256,256]{2,1,0:T(8,128)} async-done(((f32[8,256,256]{2,1,0:T(8,128)}), f32[1,256,256]{2,1,0:T(8,128)}) %reduce-scatter.2.cloned.1.call-update) | async-done | bytes 262160 | tf_op jit(solution)/shard_map/reduce_scatter | solution.py:187
  121.6 1.1 fusion.45
  122.7 0.9 slice.72
  123.6 1.1 fusion.26
  124.7 9.3 %shard_map.113 = bf16[256,1024]{1,0:T(8,128)(2,1)S(1)} custom-call(s32[1]{0:T(128)} %dynamic_slice.78.length_ref, f32[256,1024]{1,0:T(8,128)S(1)} %fusion.10.q_ref, f32[256,128]{1,0:T(8,128)S(1)} %get-tuple-element.12.cos_ref, f32[256,128]{1,0:T(8,128)S(1)} %get-tuple-element.3.sin_ref, bf16[3072,256]{1,0:T(8,128)(2,1)S(1)} %bitcast.127, ...), custom_call_target="tpu_custom_call" | custom-call | flops 3489660928 | bytes 1572864 | tf_op jit(solution)/shard_map/pallas_call | solution.py:91
  134.0 5.7 %fusion.7 = bf16[256,4096]{1,0:T(8,128)(2,1)S(1)} fusion(bf16[256,1024]{1,0:T(8,128)(2,1)S(1)} %shard_map.113, bf16[1024,8192]{1,0:T(8,128)(2,1)} %param.14), kind=kOutput, calls=%fused_computation.8 | convolution fusion | flops 2148532224 | bytes 11010048 | tf_op jit(solution)/shard_map/dot_general | solution.py:207
  139.8 1.3 copy-done.2
  141.1 1.0 dynamic-slice_bitcast_fusion
  142.1 0.6 gather_fusion.2
  142.7 0.8 bitcast_select_fusion
  143.5 23.2 %all-to-all-start.1 = ((bf16[32,16,256]{2,1,0:T(8,128)(2,1)}), bf16[32,16,256]{2,1,0:T(8,128)(2,1)S(1)}, u32[]{:S(2)}, u32[]{:S(2)}) async-start(bf16[32,16,256]{2,1,0:T(8,128)(2,1)} %bitcast_select_fusion), calls=%async_computation.2 | async-start | bytes 524288 | tf_op jit(solution)/shard_map/all_to_all | solution.py:238
  166.7 5.7 %fusion.4 = bf16[256,4096]{1,0:T(8,128)(2,1)S(1)} fusion(bf16[256,1024]{1,0:T(8,128)(2,1)S(1)} %shard_map.113, bf16[1024,8192]{1,0:T(8,128)(2,1)} %param.14), kind=kOutput, calls=%fused_computation.7 | convolution fusion | flops 2148532224 | bytes 11010048 | tf_op jit(solution)/shard_map/dot_general | solution.py:207
  172.7 4.4 %all-to-all-done.1 = bf16[32,16,256]{2,1,0:T(8,128)(2,1)S(1)} async-done(((bf16[32,16,256]{2,1,0:T(8,128)(2,1)}), bf16[32,16,256]{2,1,0:T(8,128)(2,1)S(1)}, u32[]{:S(2)}, u32[]{:S(2)}) %all-to-all-start.1) | async-done | bytes 262176 | tf_op jit(solution)/shard_map/all_to_all | solution.py:238
  177.1 0.8 reshape.305
  177.9 1.1 copy.29
  179.0 0.8 reshape.306
  179.8 1.8 fusion.12
  181.8 1.0 collective-permute-start.8
  182.7 0.9 collective-permute-start.6
  183.7 1.6 fusion.13
  185.4 0.6 collective-permute-start.3
  186.0 1.8 collective-permute-start.1
  187.8 3.2 %collective-permute-done.8 = bf16[2,32,2048]{2,1,0:T(8,128)(2,1)S(1)} collective-permute-done((bf16[2,32,2048]{2,1,0:T(8,128)(2,1)S(1)}, bf16[2,32,2048]{2,1,0:T(8,128)(2,1)S(1)}, u32[]{:S(2)}, u32[]{:S(2)}) %collective-permute-start.8) | collective-permute-done | bytes 262176 | tf_op jit(solution)/shard_map/ppermute | solution.py:116
  191.3 0.3 collective-permute-done.6
  191.8 1.5 collective-permute-start.7
  193.3 3.3 %collective-permute-done.3 = bf16[2,32,2048]{2,1,0:T(8,128)(2,1)S(1)} collective-permute-done((bf16[2,32,2048]{2,1,0:T(8,128)(2,1)S(1)}, bf16[2,32,2048]{2,1,0:T(8,128)(2,1)S(1)}, u32[]{:S(2)}, u32[]{:S(2)}) %collective-permute-start.3) | collective-permute-done | bytes 262176 | tf_op jit(solution)/shard_map/ppermute | solution.py:116
  197.2 1.8 collective-permute-start.2
  198.9 0.6 collective-permute-done.9
  199.6 2.1 %collective-permute-done.4 = bf16[32,2048]{1,0:T(8,128)(2,1)S(1)} collective-permute-done((bf16[32,2048]{1,0:T(8,128)(2,1)S(1)}, bf16[32,2048]{1,0:T(8,128)(2,1)S(1)}, u32[]{:S(2)}, u32[]{:S(2)}) %collective-permute-start.4) | collective-permute-done | bytes 131104 | tf_op jit(solution)/shard_map/ppermute | solution.py:116
  201.8 0.4 collective-permute-done.2
  202.3 0.9 fusion.14
  (66 shorter events, 3.5 us)
Async XLA Ops:
  7.2 22.6 %copy-start = (s32[4,2]{0,1:T(2,128)S(1)}, s32[4,2]{0,1:T(2,128)}, u32[]{:S(2)}) copy-start(s32[4,2]{0,1:T(2,128)} %param.19) | copy-start | bytes 100
  7.2 2.6 %copy-start.4 = (s32[4,24]{1,0:T(4,128)S(1)}, s32[4,24]{1,0:T(4,128)}, u32[]{:S(2)}) copy-start(s32[4,24]{1,0:T(4,128)} %param.17) | copy-start | bytes 1156
  7.2 2.8 %copy-start.5 = (s32[4,24]{1,0:T(4,128)S(1)}, s32[4,24]{1,0:T(4,128)}, u32[]{:S(2)}) copy-start(s32[4,24]{1,0:T(4,128)} %param.18) | copy-start | bytes 1156
  7.2 67.4 %all-gather.3.cloned.1.call-start = ((), (), s32[]{:S(2)}) async-start(), calls=%async_computation.4 | async-start | bytes 4718592 | tf_op jit(solution)/shard_map/all_gather | solution.py:179
  22.2 78.8 %all-to-all-start = ((bf16[32,192,256]{2,1,0:T(8,128)(2,1)}), bf16[32,192,256]{2,1,0:T(8,128)(2,1)}, u32[]{:S(2)}, u32[]{:S(2)}) async-start(bf16[32,192,256]{2,1,0:T(8,128)(2,1)} %reshape_reshape_broadcast_in_dim.3), calls=%async_computation | async-start | bytes 6291456 | tf_op jit(solution)/shard_map/all_to_all | solution.py:177
  29.6 92.1 %reduce-scatter.2.cloned.1.call-start = ((), (), s32[]{:S(2)}) async-start(), calls=%async_computation.3 | async-start | bytes 2359296 | tf_op jit(solution)/shard_map/reduce_scatter | solution.py:187
  79.7 3.0 %copy-start.6 = (s32[4]{0:T(128)S(1)}, s32[4]{0:T(128)}, u32[]{:S(2)}) copy-start(s32[4]{0:T(128)} %param.16) | copy-start | bytes 52
  139.7 1.3 copy-start.2
  142.1 37.7 %collective-permute-start.5 = (bf16[2,2,32,4096]{3,2,1,0:T(8,128)(2,1)}, bf16[2,2,32,4096]{3,2,1,0:T(8,128)(2,1)}, u32[]{:S(2)}, u32[]{:S(2)}) collective-permute-start(bf16[2,2,32,4096]{3,2,1,0:T(8,128)(2,1)} %dynamic-slice_bitcast_fusion), channel_id=1, source_target_pairs={{0,1},{1,0},{2,3},{3,2},{4,5},{5,4},{6,7},{7,6},{8,9},{9,8},{10,11... | collective-permute-start | bytes 3145736 | tf_op jit(solution)/shard_map/ppermute | solution.py:116
  143.5 33.6 %all-to-all-start.1 = ((bf16[32,16,256]{2,1,0:T(8,128)(2,1)}), bf16[32,16,256]{2,1,0:T(8,128)(2,1)S(1)}, u32[]{:S(2)}, u32[]{:S(2)}) async-start(bf16[32,16,256]{2,1,0:T(8,128)(2,1)} %bitcast_select_fusion), calls=%async_computation.2 | async-start | bytes 524288 | tf_op jit(solution)/shard_map/all_to_all | solution.py:238
  172.6 11.1 %collective-permute-start = (bf16[2,2,32,4096]{3,2,1,0:T(8,128)(2,1)S(1)}, bf16[2,2,32,4096]{3,2,1,0:T(8,128)(2,1)}, u32[]{:S(2)}, u32[]{:S(2)}) collective-permute-start(bf16[2,2,32,4096]{3,2,1,0:T(8,128)(2,1)S(1)} %dynamic-slice_bitcast_fusion.1), channel_id=1, source_target_pairs={{0,1},{1,0},{2,3},{3,2},{4,5},{5,4},{6,7},{7,6},{8,9},{9,8},{10,11... | collective-permute-start | bytes 3145736 | tf_op jit(solution)/shard_map/ppermute | solution.py:116
  181.8 9.2 %collective-permute-start.8 = (bf16[2,32,2048]{2,1,0:T(8,128)(2,1)S(1)}, bf16[2,32,2048]{2,1,0:T(8,128)(2,1)S(1)}, u32[]{:S(2)}, u32[]{:S(2)}) collective-permute-start(bf16[2,32,2048]{2,1,0:T(8,128)(2,1)S(1)} %dynamic-slice_bitcast_fusion.2), channel_id=1, source_target_pairs={{0,4},{1,5},{2,6},{3,7},{4,0},{5,1},{6,2},{7,3},{8,12},{9,13},{10,... | collective-permute-start | bytes 786440 | tf_op jit(solution)/shard_map/ppermute | solution.py:116
  182.7 8.9 %collective-permute-start.6 = (bf16[2,32,2048]{2,1,0:T(8,128)(2,1)S(1)}, bf16[2,32,2048]{2,1,0:T(8,128)(2,1)S(1)}, u32[]{:S(2)}, u32[]{:S(2)}) collective-permute-start(bf16[2,32,2048]{2,1,0:T(8,128)(2,1)S(1)} %dynamic-slice_bitcast_fusion.3), channel_id=1, source_target_pairs={{0,2},{1,3},{2,0},{3,1},{4,6},{5,7},{6,4},{7,5},{8,10},{9,11},{10,... | collective-permute-start | bytes 786440 | tf_op jit(solution)/shard_map/ppermute | solution.py:116
  185.4 11.3 %collective-permute-start.3 = (bf16[2,32,2048]{2,1,0:T(8,128)(2,1)S(1)}, bf16[2,32,2048]{2,1,0:T(8,128)(2,1)S(1)}, u32[]{:S(2)}, u32[]{:S(2)}) collective-permute-start(bf16[2,32,2048]{2,1,0:T(8,128)(2,1)S(1)} %dynamic-slice_bitcast_fusion.4), channel_id=1, source_target_pairs={{0,4},{1,5},{2,6},{3,7},{4,0},{5,1},{6,2},{7,3},{8,12},{9,13},{10,... | collective-permute-start | bytes 786440 | tf_op jit(solution)/shard_map/ppermute | solution.py:116
  186.0 11.1 %collective-permute-start.1 = (bf16[2,32,2048]{2,1,0:T(8,128)(2,1)S(1)}, bf16[2,32,2048]{2,1,0:T(8,128)(2,1)S(1)}, u32[]{:S(2)}, u32[]{:S(2)}) collective-permute-start(bf16[2,32,2048]{2,1,0:T(8,128)(2,1)S(1)} %dynamic-slice_bitcast_fusion.5), channel_id=1, source_target_pairs={{0,2},{1,3},{2,0},{3,1},{4,6},{5,7},{6,4},{7,5},{8,10},{9,11},{10,... | collective-permute-start | bytes 786440 | tf_op jit(solution)/shard_map/ppermute | solution.py:116
  191.1 11.1 %copy-start.3 = (bf16[1,32,8192]{2,1,0:T(8,128)(2,1)S(1)}, bf16[1,32,8192]{2,1,0:T(8,128)(2,1)}, u32[]{:S(2)}) copy-start(bf16[1,32,8192]{2,1,0:T(8,128)(2,1)} %param.11) | copy-start | bytes 1572868
  191.1 8.4 %collective-permute-start.9 = (bf16[32,2048]{1,0:T(8,128)(2,1)S(1)}, bf16[32,2048]{1,0:T(8,128)(2,1)S(1)}, u32[]{:S(2)}, u32[]{:S(2)}) collective-permute-start(bf16[32,2048]{1,0:T(8,128)(2,1)S(1)} %fusion.24), channel_id=1, source_target_pairs={{0,2},{1,3},{2,0},{3,1},{4,6},{5,7},{6,4},{7,5},{8,10},{9,11},{10,... | collective-permute-start | bytes 393224 | tf_op jit(solution)/shard_map/ppermute | solution.py:116
  191.8 7.8 %collective-permute-start.7 = (bf16[32,2048]{1,0:T(8,128)(2,1)S(1)}, bf16[32,2048]{1,0:T(8,128)(2,1)S(1)}, u32[]{:S(2)}, u32[]{:S(2)}) collective-permute-start(bf16[32,2048]{1,0:T(8,128)(2,1)S(1)} %fusion.23), channel_id=1, source_target_pairs={{0,4},{1,5},{2,6},{3,7},{4,0},{5,1},{6,2},{7,3},{8,12},{9,13},{10,... | collective-permute-start | bytes 393224 | tf_op jit(solution)/shard_map/ppermute | solution.py:116
  196.6 6.5 %copy-start.1 = (s32[4,2]{0,1:T(2,128)S(1)}, s32[4,2]{0,1:T(2,128)}, u32[]{:S(2)}) copy-start(s32[4,2]{0,1:T(2,128)} %param.19) | copy-start | bytes 100
  196.7 5.0 %collective-permute-start.4 = (bf16[32,2048]{1,0:T(8,128)(2,1)S(1)}, bf16[32,2048]{1,0:T(8,128)(2,1)S(1)}, u32[]{:S(2)}, u32[]{:S(2)}) collective-permute-start(bf16[32,2048]{1,0:T(8,128)(2,1)S(1)} %fusion.22), channel_id=1, source_target_pairs={{0,2},{1,3},{2,0},{3,1},{4,6},{5,7},{6,4},{7,5},{8,10},{9,11},{10,... | collective-permute-start | bytes 393224 | tf_op jit(solution)/shard_map/ppermute | solution.py:116
  197.2 5.0 %collective-permute-start.2 = (bf16[32,2048]{1,0:T(8,128)(2,1)S(1)}, bf16[32,2048]{1,0:T(8,128)(2,1)S(1)}, u32[]{:S(2)}, u32[]{:S(2)}) collective-permute-start(bf16[32,2048]{1,0:T(8,128)(2,1)S(1)} %fusion.21), channel_id=1, source_target_pairs={{0,4},{1,5},{2,6},{3,7},{4,0},{5,1},{6,2},{7,3},{8,12},{9,13},{10,... | collective-permute-start | bytes 393224 | tf_op jit(solution)/shard_map/ppermute | solution.py:116
Sparse Core Ops, SparseCore 0:
  9.9 64.6 all-gather.2
  82.6 39.0 reduce-scatter.1

commit v2 on v1

v2 whole, which is shorter than its diff:
```python
import functools
import math

import jax
import jax.numpy as jnp
from jax import lax
from jax.experimental import pallas as pl
from jax.experimental.pallas import tpu as pltpu
from jax.sharding import PartitionSpec as P

KVH = 8
HD = 128
BLK = 128
LOG2E = 1.4426950408889634


def frequencies(width):
    half_width = width // 2
    base_freq = jnp.power(
        jnp.float32(500000.0), -jnp.arange(half_width, dtype=jnp.float32) * (2.0 / width)
    )
    wavelength = 2.0 * math.pi / base_freq
    blended = (8192.0 / wavelength - 1.0) / 3.0
    middle = (1.0 - blended) * base_freq / 8.0 + blended * base_freq
    return jnp.where(
        wavelength < 2048.0, base_freq, jnp.where(wavelength > 8192.0, base_freq / 8.0, middle)
    )


def rope_tables(positions):
    angles = positions.astype(jnp.float32)[:, None] * frequencies(HD)[None, :]
    cosine, sine = jnp.cos(angles), jnp.sin(angles)
    return jnp.concatenate([cosine, cosine], axis=1), jnp.concatenate([-sine, sine], axis=1)


def pack_kernel(heads_share, group_ref, holder_ref, slot_ref, pool_ref, out_ref):
    key_width = KVH * HD
    for request in range(holder_ref.shape[0]):

        def one(index, count):
            mine = holder_ref[request, index] == group_ref[0]

            @pl.when(mine)
            def _():
                rows = pool_ref[slot_ref[request, index]]
                for dest in range(out_ref.shape[1]):
                    at = dest // heads_share * HD
                    out_ref[request, dest, count] = jnp.concatenate(
                        [rows[:, at : at + HD], rows[:, key_width + at : key_width + at + HD]],
                        axis=1,
                    )

            return count + mine.astype(jnp.int32)

        lax.fori_loop(0, holder_ref.shape[1], one, jnp.int32(0))


def pack(group, hit_holder, hit_slot, kv_pool, cp_count, holder_cap):
    requests = hit_holder.shape[0]
    block_rows = kv_pool.shape[1]
    shape = (requests, cp_count, holder_cap, block_rows, 2 * HD)
    return pl.pallas_call(
        functools.partial(pack_kernel, cp_count // KVH),
        grid_spec=pltpu.PrefetchScalarGridSpec(
            num_scalar_prefetch=3,
            grid=(1,),
            in_specs=[pl.BlockSpec(kv_pool.shape, lambda i, *_: (0, 0, 0))],
            out_specs=pl.BlockSpec(shape, lambda i, *_: (0, 0, 0, 0, 0)),
        ),
        out_shape=jax.ShapeDtypeStruct(shape, kv_pool.dtype),
        compiler_params=pltpu.CompilerParams(vmem_limit_bytes=24 * 1024 * 1024),
    )(group, hit_holder, hit_slot, kv_pool)


def attention_kernel(
    tile, ordered, length_ref, group_ref, holder_ref,
    q_ref, cos_ref, sin_ref, arrived_ref, fresh_ref, out_ref, prefix_ref,
):
    group = group_ref[0]
    span = prefix_ref.shape[0]
    _, ranks, _, block_rows, _ = arrived_ref.shape
    blocks = holder_ref.shape[1]
    row0 = pl.program_id(1) * tile

    @pl.when((pl.program_id(0) == 0) & (pl.program_id(1) == 0))
    def _():
        def place(index, counts):
            if ordered:
                holder, rank = 0, index
            else:
                holder = holder_ref[group, index]
                rank = sum(jnp.where(holder == h, counts[h], 0) for h in range(len(counts)))
            for r in range(ranks):
                at = pl.multiple_of(index * (ranks * block_rows), ranks * block_rows)
                prefix_ref[pl.ds(at + r * block_rows, block_rows), :] = arrived_ref[holder, r, rank]
            return tuple(
                n + (holder == h).astype(jnp.int32) if not ordered else n
                for h, n in enumerate(counts)
            )

        lax.fori_loop(0, blocks, place, (jnp.int32(0),) * holder_ref.shape[0])

    seen = lax.broadcasted_iota(jnp.int32, (1, span), 1) < length_ref[group]
    bias = jnp.where(seen, 0.0, -1e30)
    columns = lax.broadcasted_iota(jnp.int32, (tile, fresh_ref.shape[0]), 1)
    rows = lax.broadcasted_iota(jnp.int32, (tile, fresh_ref.shape[0]), 0) + row0
    causal = columns <= rows
    factor = HD ** (-0.5) * LOG2E

    def scores(query, keys):
        return lax.dot_general(
            query, keys, (((1,), (1,)), ((), ())), preferred_element_type=jnp.float32
        )

    for head in range(q_ref.shape[1] // HD):
        lanes = slice(head * HD, (head + 1) * HD)
        raw = q_ref[:, lanes]
        query = raw * cos_ref[...] + pltpu.roll(raw, HD // 2, 1) * sin_ref[...]
        query = (query * factor).astype(jnp.bfloat16)
        old = scores(query, prefix_ref[:, :HD]) + bias
        new = jnp.where(causal, scores(query, fresh_ref[:, :HD]), -1e30)
        peak = jnp.maximum(
            jnp.max(old, axis=1, keepdims=True), jnp.max(new, axis=1, keepdims=True)
        )
        old, new = jnp.exp2(old - peak), jnp.exp2(new - peak)
        total = jnp.sum(old, axis=1, keepdims=True) + jnp.sum(new, axis=1, keepdims=True)
        mixed = jnp.dot(
            old.astype(jnp.bfloat16), prefix_ref[:, HD:], preferred_element_type=jnp.float32
        ) + jnp.dot(
            new.astype(jnp.bfloat16), fresh_ref[:, HD:], preferred_element_type=jnp.float32
        )
        out_ref[:, lanes] = (mixed / total).astype(jnp.bfloat16)


def attention(prefix_len, group, hit_holder, raw_queries, cosine, sine, arrived, fresh, ordered):
    rows, width = raw_queries.shape
    tile = min(256, rows)
    span = hit_holder.shape[1] * BLK
    keys = span + rows
    return pl.pallas_call(
        functools.partial(attention_kernel, tile, ordered),
        grid_spec=pltpu.PrefetchScalarGridSpec(
            num_scalar_prefetch=3,
            grid=(width // (2 * HD), rows // tile),
            in_specs=[
                pl.BlockSpec((tile, 2 * HD), lambda h, t, *_: (t, h)),
                pl.BlockSpec((tile, HD), lambda h, t, *_: (t, 0)),
                pl.BlockSpec((tile, HD), lambda h, t, *_: (t, 0)),
                pl.BlockSpec(arrived.shape, lambda h, t, *_: (0, 0, 0, 0, 0)),
                pl.BlockSpec(fresh.shape, lambda h, t, *_: (0, 0)),
            ],
            out_specs=pl.BlockSpec((tile, 2 * HD), lambda h, t, *_: (t, h)),
            scratch_shapes=[pltpu.VMEM((span, 2 * HD), jnp.bfloat16)],
        ),
        out_shape=jax.ShapeDtypeStruct((rows, width), jnp.bfloat16),
        compiler_params=pltpu.CompilerParams(vmem_limit_bytes=40 * 1024 * 1024),
        cost_estimate=pl.CostEstimate(
            flops=4 * rows * width * keys,
            bytes_accessed=rows * width * 6,
            transcendentals=rows * width // HD * keys,
        ),
    )(prefix_len, group, hit_holder, raw_queries, cosine, sine, arrived, fresh)


def stacked(refs, last):
    whole, low, high = refs[:6], refs[6:8], refs[8:10]
    tail = [jnp.where(last, h[...], l[...]) for l, h in zip(low, high)]
    return jnp.concatenate([r[...] for r in whole] + tail, axis=0)


def keyval_kernel(rank_ref, *refs):
    parts, weight_ref, out_ref = refs[:10], refs[10], refs[11]
    rank = rank_ref[0]
    rows = parts[0].shape[0]
    tokens = stacked(parts, rank >= 4)
    key_width = KVH * HD
    for head in range(KVH):
        for half in range(2):
            at = half * key_width + head * HD
            product = jnp.dot(
                tokens, weight_ref[:, at : at + HD], preferred_element_type=jnp.float32
            )
            for b in range(8):
                to = pl.multiple_of((rank ^ b) * rows, rows)
                out_ref[head, pl.ds(to, rows), half * HD : (half + 1) * HD] = product[
                    b * rows : (b + 1) * rows
                ]


def query_kernel(rank_ref, *refs):
    parts, weight_ref, out_ref, total_ref = refs[:10], refs[10], refs[11], refs[12]
    step = pl.program_id(0)
    rank = rank_ref[0]
    rows = parts[0].shape[0]
    tokens = stacked(parts, step >= 4)

    @pl.when(step == 0)
    def _():
        total_ref[...] = jnp.zeros_like(total_ref)

    total_ref[...] += jnp.dot(tokens, weight_ref[...], preferred_element_type=jnp.float32)

    @pl.when(step == pl.num_programs(0) - 1)
    def _():
        for b in range(8):
            to = pl.multiple_of((rank ^ b) * rows, rows)
            out_ref[pl.ds(to, rows), :] = total_ref[b * rows : (b + 1) * rows]


def part_specs(rows, depth, block):
    whole = pl.BlockSpec((rows, depth), lambda i, r: (0, block(i, r)))
    low = pl.BlockSpec((rows, depth), lambda i, r: (0, jnp.minimum(block(i, r), 3)))
    high = pl.BlockSpec((rows, depth), lambda i, r: (0, jnp.maximum(block(i, r) - 4, 0)))
    return [whole] * 6 + [low] * 2 + [high] * 2


def keyval_project(rank, parts, w_keyval):
    rows = parts[0].shape[0]
    depth, width = w_keyval.shape
    shape = (KVH, 8 * rows, 2 * HD)
    return pl.pallas_call(
        keyval_kernel,
        grid_spec=pltpu.PrefetchScalarGridSpec(
            num_scalar_prefetch=1,
            grid=(1,),
            in_specs=part_specs(rows, depth, lambda i, r: r[0])
            + [pl.BlockSpec((depth, width), lambda i, r: (0, 0))],
            out_specs=pl.BlockSpec(shape, lambda i, r: (0, 0, 0)),
        ),
        out_shape=jax.ShapeDtypeStruct(shape, jnp.float32),
        compiler_params=pltpu.CompilerParams(vmem_limit_bytes=24 * 1024 * 1024),
        cost_estimate=pl.CostEstimate(
            flops=16 * rows * depth * width, bytes_accessed=2 * depth * width, transcendentals=0
        ),
    )(rank, *parts, w_keyval)


def query_project(rank, parts, w_query):
    rows, depth = parts[0].shape
    width = w_query.shape[1]
    block = depth // 8
    return pl.pallas_call(
        query_kernel,
        grid_spec=pltpu.PrefetchScalarGridSpec(
            num_scalar_prefetch=1,
            grid=(8,),
            in_specs=part_specs(rows, block, lambda i, r: i)
            + [pl.BlockSpec((block, width), lambda i, r: (i, 0))],
            out_specs=pl.BlockSpec((8 * rows, width), lambda i, r: (0, 0)),
            scratch_shapes=[pltpu.VMEM((8 * rows, width), jnp.float32)],
        ),
        out_shape=jax.ShapeDtypeStruct((8 * rows, width), jnp.float32),
        compiler_params=pltpu.CompilerParams(vmem_limit_bytes=24 * 1024 * 1024),
        cost_estimate=pl.CostEstimate(
            flops=16 * rows * depth * width, bytes_accessed=2 * depth * width, transcendentals=0
        ),
    )(rank, *parts, w_query)


def gather_parts(own):
    half = own.shape[1] // 2
    near_x, near_y, near_core = swap(own, 2, 8), swap(own, 4, 8), swap(own, 1, 8)
    left = swap(near_y[:, :half], 2, 8)
    right = swap(near_x[:, half:], 4, 8)
    return [
        own, near_core, near_x, swap(near_x, 1, 8), near_y, swap(near_y, 1, 8),
        left, swap(left, 1, 8), right, swap(right, 1, 8),
    ]


def swap(array, bit, count):
    return lax.ppermute(array, "cp", [(i, i ^ bit) for i in range(count)])


def pick(array, index, axis):
    return lax.dynamic_index_in_dim(array, index, axis, keepdims=False)


def add(one, two):
    return one.astype(jnp.float32) + two.astype(jnp.float32)


def scatter_sum(part, rank):
    rows, width = part.shape
    core, x, y = rank % 2, rank // 2 % 2, rank // 4
    view = part.reshape(2, 2, 2, rows // 8, width)
    got = swap(pick(view, 1 - core, 2), 1, 8)
    pair = add(pick(view, core, 2), got).astype(jnp.bfloat16)
    half = width // 2
    one, two = pair[..., :half], pair[..., half:]
    got_one = swap(pick(one, 1 - x, 1), 2, 8)
    got_two = swap(pick(two, 1 - y, 0), 4, 8)
    one = add(pick(one, x, 1), got_one)
    two = add(pick(two, y, 0), got_two)
    end_one = swap(pick(one, 1 - y, 0).astype(jnp.bfloat16), 4, 8)
    end_two = swap(pick(two, 1 - x, 0).astype(jnp.bfloat16), 2, 8)
    one = add(pick(one, y, 0), end_one)
    two = add(pick(two, x, 0), end_two)
    return jnp.concatenate([one, two], axis=1)


def local(
    hidden, residual, w_query, w_keyval, w_out, kv_pool, prefix_len, hit_holder, hit_slot, owner
):
    cp_count = lax.axis_size("cp")
    group_id = lax.axis_index("req")
    cp_rank = lax.axis_index("cp")
    tok_rows = hidden.shape[1]
    stretch_rows = tok_rows * cp_count
    slice_rows = w_keyval.shape[0]
    block_rows = kv_pool.shape[1]
    request_count = hit_holder.shape[0]
    prefix_blocks = hit_holder.shape[1]
    new_blocks = owner.shape[1]
    owner_cap = (new_blocks + 1) // 2
    holder_cap = prefix_blocks // 2
    heads_share = cp_count // KVH
    length = prefix_len[group_id]
    positions = length + jnp.arange(stretch_rows, dtype=jnp.int32)
    cosine, sine = rope_tables(positions)

    group = group_id.reshape(1)
    rank = cp_rank.reshape(1)
    tiled = block_rows % 16 == 0
    if tiled:
        sending = pack(group, hit_holder, hit_slot, kv_pool, cp_count, holder_cap)
    else:
        slot_ids = jnp.arange(holder_cap, dtype=jnp.int32)
        holds_hit = hit_holder == group_id
        hit_order = jnp.cumsum(holds_hit.astype(jnp.int32), axis=1) - 1
        picked = holds_hit[:, None, :] & (hit_order[:, None, :] == slot_ids[None, :, None])
        sources = jnp.sum(jnp.where(picked, hit_slot[:, None, :], 0), axis=2)
        by_head = kv_pool.reshape(-1, block_rows, 2, KVH, HD)[sources]
        by_head = jnp.transpose(by_head, (0, 4, 1, 2, 3, 5))
        sending = jnp.repeat(by_head, heads_share, axis=1)
    sending = sending.reshape(request_count * cp_count, holder_cap * block_rows, 2 * HD)
    arrived = lax.all_to_all(sending, ("req", "cp"), split_axis=0, concat_axis=0, tiled=True)
    arrived = arrived.reshape(request_count, cp_count, holder_cap, block_rows, 2 * HD)

    if cp_count == 8:
        parts = gather_parts(hidden[0])
        partial_kv = keyval_project(rank, parts, w_keyval)
        raw_queries = query_project(rank, parts, w_query)
    else:
        gathered = lax.all_gather(hidden[0], "cp", axis=0, tiled=True)
        raw_queries = jnp.dot(gathered, w_query, preferred_element_type=jnp.float32)
        columns = lax.dynamic_slice_in_dim(gathered, cp_rank * slice_rows, slice_rows, 1)
        partial_kv = jnp.dot(columns, w_keyval, preferred_element_type=jnp.float32)
        partial_kv = jnp.transpose(
            partial_kv.reshape(stretch_rows, 2, KVH, HD), (2, 0, 1, 3)
        ).reshape(KVH, stretch_rows, 2 * HD)
        partial_kv = jnp.repeat(partial_kv, heads_share, axis=0)
    summed = lax.psum_scatter(partial_kv, "cp", scatter_dimension=0, tiled=True)[0]
    keys = summed[:, :HD]
    keys = keys * cosine + jnp.roll(keys, HD // 2, axis=1) * sine
    fresh = jnp.concatenate([keys, summed[:, HD:]], axis=1).astype(jnp.bfloat16)

    if not tiled:
        my_holders = hit_holder[group_id]
        hit_index = jnp.arange(prefix_blocks, dtype=jnp.int32)
        earlier = (my_holders[:, None] == my_holders[None, :]) & (
            hit_index[:, None] > hit_index[None, :]
        )
        hit_rank = jnp.sum(earlier.astype(jnp.int32), axis=1)
        arrived = arrived[my_holders, :, hit_rank].reshape(1, 1, prefix_blocks, BLK, 2 * HD)

    attended = attention(
        prefix_len, group, hit_holder, raw_queries, cosine, sine, arrived, fresh, not tiled
    )

    if cp_count == 8:
        wide = w_out.shape[1] // 2
        sums = [
            scatter_sum(
                jnp.dot(
                    attended, w_out[:, at : at + wide], preferred_element_type=jnp.float32
                ).astype(jnp.bfloat16),
                cp_rank,
            )
            for at in range(0, w_out.shape[1], wide)
        ]
        projected = jnp.concatenate(sums, axis=1)
    else:
        projected = lax.psum_scatter(
            jnp.dot(attended, w_out, preferred_element_type=jnp.float32).astype(jnp.bfloat16),
            "cp",
            scatter_dimension=0,
            tiled=True,
        ).astype(jnp.float32)
    layer_out = (residual[0].astype(jnp.float32) + projected).astype(jnp.bfloat16)[None]

    my_owners = owner[group_id]
    block_ids = jnp.arange(new_blocks, dtype=jnp.int32)
    before = (my_owners[:, None] == my_owners[None, :]) & (block_ids[:, None] > block_ids[None, :])
    owner_rank = jnp.sum(before.astype(jnp.int32), axis=1)
    targets = jnp.arange(request_count, dtype=jnp.int32)[:, None, None]
    cap_ids = jnp.arange(owner_cap, dtype=jnp.int32)[None, :, None]
    chosen = (my_owners[None, None, :] == targets) & (owner_rank[None, None, :] == cap_ids)
    block_pick = jnp.sum(jnp.where(chosen, block_ids[None, None, :], 0), axis=2)
    present = jnp.any(chosen, axis=2)
    blocks = fresh.reshape(new_blocks, cp_count, block_rows, 2 * HD)[block_pick]
    blocks = jnp.where(present[:, :, None, None, None], blocks, jnp.zeros((), jnp.bfloat16))
    blocks = jnp.transpose(blocks, (0, 2, 1, 3, 4)).reshape(
        request_count * cp_count, owner_cap * block_rows, 2 * HD
    )
    landed = lax.all_to_all(blocks, ("req", "cp"), split_axis=0, concat_axis=0, tiled=True)
    landed = landed.reshape(request_count, cp_count, owner_cap, block_rows, 2, HD)[:, ::heads_share]
    new_cache = jnp.transpose(landed, (0, 2, 3, 4, 1, 5)).reshape(
        1, request_count * owner_cap, block_rows, 2 * KVH * HD
    )
    return (layer_out, new_cache)


def solution(mesh):
    in_specs = (
        P("req", "cp", None),
        P("req", "cp", None),
        P(None, "cp"),
        P("cp", None),
        P("cp", None),
        P("req", "cp", None),
        P(),
        P(),
        P(),
        P(),
    )
    out_specs = (P("req", "cp", None), P("req", None, "cp", None))
    return jax.shard_map(local, mesh=mesh, in_specs=in_specs, out_specs=out_specs, check_vma=False)
```

time: 211 us -> 237 us (1.12)
  waiting for transfers between devices: 84.2 us -> 124 us
  Pallas kernels: 9.25 us -> 32.1 us
  matrix products: 24.6 us -> 8.28 us
  starting transfers between devices: 39.1 us -> 27.5 us
  local copies, waits for them, and re-layouts: 29.7 us -> 23.4 us
  other arithmetic: 8.79 us -> 5.89 us
    all_gather x1 -> x0, waiting for transfers between devices: 44.6 us -> none  [local(): gathered = lax.all_gather(hidden[0], 'cp', axis=0, tiled=True)]
    all_to_all x1, waiting for transfers between devices: 15.8 us -> 52.8 us  [local(): lax.all_to_all(sending, ('req', 'cp'), split_axis=0, concat_axis=0, tiled...]
    reduce_scatter x1, waiting for transfers between devices: 8.44 us -> 38.5 us  [local(): lax.psum_scatter(partial_kv, 'cp', scatter_dimension=0, tiled=True)[0]]
    pallas_call x1 -> x4, Pallas kernels: 9.25 us -> 32.1 us  [the longest x1 15.4 us: attention(): pl.pallas_call(functools.partial(attention_kernel, tile, ordered), grid_s...]
    all_to_all x1, starting transfers between devices: 23.2 us -> 4.61 us  [local(): lax.all_to_all(blocks, ('req', 'cp'), split_axis=0, concat_axis=0, tiled=...]
    ppermute x10 -> x19, waiting for transfers between devices: 10.1 us -> 27.4 us  [swap(): return lax.ppermute(array, 'cp', [(i, i ^ bit) for i in range(count)])]
    unnamed x16 -> x54, local copies, waits for them, and re-layouts: 3.56 us -> 17.4 us
    dot_general x2 -> x0, matrix products: 13.1 us -> none  [the longest x1 9.49 us: local(): raw_queries = jnp.dot(gathered, w_query, preferred_element_type=jnp.float32)]
  transfers between devices with their start and end apart: 14 -> 22, of which waited for: 11 -> 13; matrix products, arithmetic and copies ran while one was open for 24% -> 3% of each run, Pallas kernels for 0% -> 5%
where the time goes in v2:
time: 237 us; the launch traced here: 236 us
  waiting for transfers between devices  124 us (52%)
  Pallas kernels  32.1 us (14%)
  starting transfers between devices  27.5 us (12%)
  local copies, waits for them, and re-layouts  23.4 us (10%)
  between operations  14.6 us (6%)
  matrix products  8.28 us (3%)
  other arithmetic  5.89 us (2%)
    all_to_all x1, waiting for transfers between devices, local(): lax.all_to_all(sending, ('req', 'cp'), split_axis=0, concat_axis=0, tiled...  52.8 us
    reduce_scatter x1, waiting for transfers between devices, local(): lax.psum_scatter(partial_kv, 'cp', scatter_dimension=0, tiled=True)[0]  38.5 us
    ppermute x19, waiting for transfers between devices, swap(): return lax.ppermute(array, 'cp', [(i, i ^ bit) for i in range(count)])  27.4 us
    ppermute x19, starting transfers between devices, swap(): return lax.ppermute(array, 'cp', [(i, i ^ bit) for i in range(count)])  19 us
    unnamed x54, local copies, waits for them, and re-layouts  17.4 us
    pallas_call x1, Pallas kernels, attention(): pl.pallas_call(functools.partial(attention_kernel, tile, ordered), grid_s...  15.4 us
    dot_general x2, matrix products, local(): jnp.dot(attended, w_out[:, at:at + wide], preferred_element_type=jnp.floa...  8.28 us
    pallas_call x1, Pallas kernels, query_project(): pl.pallas_call(query_kernel, grid_spec=pltpu.PrefetchScalarGridSpec(num_s...  7.79 us
  transfers between devices with their start and end apart: 22, of which 13 were waited for; matrix products, arithmetic and copies ran while one was open for 3% of the time, Pallas kernels for 5%

profile of v2, /device:TPU:0, one launch (start us, length us, event | category | flops | bytes accessed | tf_op | source)
XLA Modules:
  0.0 235.8 jit_solution(13320801797723895137)
XLA Ops:
  7.2 3.0 %collective-permute-start.3 = (bf16[32,8192]{1,0:T(8,128)(2,1)}, bf16[32,8192]{1,0:T(8,128)(2,1)S(1)}, u32[]{:S(2)}, u32[]{:S(2)}) collective-permute-start(bf16[32,8192]{1,0:T(8,128)(2,1)} %bitcast.92), channel_id=1, source_target_pairs={{0,4},{1,5},{2,6},{3,7},{4,0},{5,1},{6,2},{7,3},{8,12},{9,13},{10,... | collective-permute-start | bytes 1572872 | tf_op jit(solution)/shard_map/ppermute | solution.py:272
  10.3 1.5 collective-permute-start.1
  11.8 10.6 %collective-permute-done.3.refs_4_ = bf16[32,8192]{1,0:T(8,128)(2,1)S(1)} collective-permute-done((bf16[32,8192]{1,0:T(8,128)(2,1)}, bf16[32,8192]{1,0:T(8,128)(2,1)S(1)}, u32[]{:S(2)}, u32[]{:S(2)}) %collective-permute-start.3) | collective-permute-done | bytes 524320 | tf_op jit(solution)/shard_map/ppermute | solution.py:272
  22.4 1.8 collective-permute-start.5
  24.2 1.6 collective-permute-start.7
  26.3 3.7 %collective-permute-done.5.refs_6_ = bf16[32,4096]{1,0:T(8,128)(2,1)S(1)} collective-permute-done((bf16[32,4096]{1,0:T(8,128)(2,1)S(1)}, bf16[32,4096]{1,0:T(8,128)(2,1)S(1)}, u32[]{:S(2)}, u32[]{:S(2)}) %collective-permute-start.5) | collective-permute-done | bytes 262176 | tf_op jit(solution)/shard_map/ppermute | solution.py:272
  30.0 1.2 collective-permute-done.7.refs_8_
  31.5 1.3 collective-permute-done.8.refs_9_
  32.9 2.2 copy-done.3
  35.0 1.0 copy-done.4
  36.1 4.9 %shard_map.115 = f32[8,256,256]{2,1,0:T(8,128)} custom-call(s32[1]{0:T(128)} %bitcast.1.rank_ref, bf16[32,8192]{1,0:T(8,128)(2,1)S(1)} %bitcast.95, bf16[32,8192]{1,0:T(8,128)(2,1)S(1)} %collective-permute-done.refs_1_, bf16[32,8192]{1,0:T(8,128)(2,1)S(1)} %collective-permute-done.1.refs_2_, bf16[32,8192]{1,0:T(8,128)(2,1)S(1)} %collective-permute-done.2.refs_3_, ...), custom_call_target="tpu_custom_call" | custom-call | flops 1073741824 | bytes 4194304 | tf_op jit(solution)/shard_map/pallas_call | solution.py:221
  44.2 38.5 %reduce-scatter.2.cloned.1.call-done = f32[1,256,256]{2,1,0:T(8,128)} async-done(((f32[8,256,256]{2,1,0:T(8,128)}), f32[1,256,256]{2,1,0:T(8,128)}) %reduce-scatter.2.cloned.1.call-update) | async-done | bytes 262160 | tf_op jit(solution)/shard_map/reduce_scatter | solution.py:353
  82.7 1.1 fusion.30
  83.8 0.9 slice.78
  84.7 1.8 fusion.22
  87.7 0.8 bitcast_select_fusion
  88.5 4.6 %all-to-all-start.1 = ((bf16[32,16,256]{2,1,0:T(8,128)(2,1)}), bf16[32,16,256]{2,1,0:T(8,128)(2,1)S(1)}, u32[]{:S(2)}, u32[]{:S(2)}) async-start(bf16[32,16,256]{2,1,0:T(8,128)(2,1)} %bitcast_select_fusion), calls=%async_computation.2 | async-start | bytes 524288 | tf_op jit(solution)/shard_map/all_to_all | solution.py:406
  93.1 1.4 copy-done.6
  94.5 4.0 %shard_map.114 = bf16[4,8,12,16,256]{4,3,2,1,0:T(8,128)(2,1)} custom-call(s32[1]{0:T(128)} %bitcast.group_ref, s32[4,24]{1,0:T(4,128)S(1)} %copy-done.15, s32[4,24]{1,0:T(4,128)S(1)} %copy-done.14, bf16[24,16,2048]{2,1,0:T(8,128)(2,1)S(1)} %copy-done.6), custom_call_target="tpu_custom_call" | custom-call | tf_op jit(solution)/shard_map/pallas_call | solution.py:62
  98.5 5.2 %all-to-all-done.1 = bf16[32,16,256]{2,1,0:T(8,128)(2,1)S(1)} async-done(((bf16[32,16,256]{2,1,0:T(8,128)(2,1)}), bf16[32,16,256]{2,1,0:T(8,128)(2,1)S(1)}, u32[]{:S(2)}, u32[]{:S(2)}) %all-to-all-start.1) | async-done | bytes 262176 | tf_op jit(solution)/shard_map/all_to_all | solution.py:406
  103.7 0.7 copy-done.17
  104.4 3.8 %all-to-all-start = ((bf16[32,192,256]{2,1,0:T(8,128)(2,1)}), bf16[32,192,256]{2,1,0:T(8,128)(2,1)}, u32[]{:S(2)}, u32[]{:S(2)}) async-start(bf16[32,192,256]{2,1,0:T(8,128)(2,1)} %bitcast.4), calls=%async_computation | async-start | bytes 6291456 | tf_op jit(solution)/shard_map/all_to_all | solution.py:337
  108.4 5.8 %copy-done.2 = bf16[8192,1024]{1,0:T(8,128)(2,1)S(1)} copy-done((bf16[8192,1024]{1,0:T(8,128)(2,1)S(1)}, bf16[8192,1024]{1,0:T(8,128)(2,1)}, u32[]{:S(2)}) %copy-start.2) | copy-done | bytes 16777240
  114.1 0.9 copy-done.10
  115.1 0.9 copy-done.12
  116.0 7.8 %shard_map.113.q_ref = f32[256,1024]{1,0:T(8,128)S(1)} custom-call(s32[1]{0:T(128)} %bitcast.1.rank_ref, bf16[32,8192]{1,0:T(8,128)(2,1)S(1)} %bitcast.96, bf16[32,8192]{1,0:T(8,128)(2,1)S(1)} %collective-permute-done.refs_1_, bf16[32,8192]{1,0:T(8,128)(2,1)S(1)} %collective-permute-done.1.refs_2_, bf16[32,8192]{1,0:T(8,128)(2,1)S(1)} %collective-permute-done.2.refs_3_, ...), custom_call_target="tpu_custom_call" | custom-call | flops 4294967296 | bytes 16777216 | tf_op jit(solution)/shard_map/pallas_call | solution.py:242
  123.8 1.0 copy-done.7
  124.8 1.0 reshape.241
  126.0 0.8 reshape.242
  126.8 52.8 %all-to-all-done = bf16[32,192,256]{2,1,0:T(8,128)(2,1)} async-done(((bf16[32,192,256]{2,1,0:T(8,128)(2,1)}), bf16[32,192,256]{2,1,0:T(8,128)(2,1)}, u32[]{:S(2)}, u32[]{:S(2)}) %all-to-all-start) | async-done | bytes 3145760 | tf_op jit(solution)/shard_map/all_to_all | solution.py:337
  179.7 1.2 copy-done.8
  180.9 0.9 copy-done.13
  181.8 15.4 %shard_map.116 = bf16[256,1024]{1,0:T(8,128)(2,1)S(1)} custom-call(s32[4]{0:T(128)S(1)} %copy-done.16, s32[1]{0:T(128)} %bitcast.group_ref, s32[4,24]{1,0:T(4,128)S(1)} %copy-done.15, f32[256,1024]{1,0:T(8,128)S(1)} %copy-done.8, f32[256,128]{1,0:T(8,128)S(1)} %copy-done.13, f32[256,128]{1,0:T(8,128)S(1)} %get-tuple-element.3.sin_ref, ...), custom_call_target="tpu_custom_call" | custom-call | flops 3489660928 | bytes 1572864 | tf_op jit(solution)/shard_map/pallas_call | solution.py:140
  197.3 5.9 %fusion.4 = bf16[256,4096]{1,0:T(8,128)(2,1)S(1)} fusion(bf16[256,1024]{1,0:T(8,128)(2,1)S(1)} %shard_map.116, bf16[1024,8192]{1,0:T(8,128)(2,1)} %param.14), kind=kOutput, calls=%fused_computation.5 | convolution fusion | flops 2148532224 | bytes 11010048 | tf_op jit(solution)/shard_map/dot_general | solution.py:375
  203.4 2.4 %fusion.7 = bf16[256,4096]{1,0:T(8,128)(2,1)S(1)} fusion(bf16[256,1024]{1,0:T(8,128)(2,1)S(1)} %shard_map.116, bf16[1024,8192]{1,0:T(8,128)(2,1)S(1)} %bitcast.108), kind=kOutput, calls=%fused_computation.6 | convolution fusion | flops 2148532224 | bytes 11010048 | tf_op jit(solution)/shard_map/dot_general | solution.py:375
  206.8 1.2 collective-permute-start.10
  208.0 1.6 collective-permute-start.12
  210.5 1.3 collective-permute-start.17
  211.8 4.2 %collective-permute-done.10 = bf16[2,32,2048]{2,1,0:T(8,128)(2,1)S(1)} collective-permute-done((bf16[2,32,2048]{2,1,0:T(8,128)(2,1)S(1)}, bf16[2,32,2048]{2,1,0:T(8,128)(2,1)S(1)}, u32[]{:S(2)}, u32[]{:S(2)}) %collective-permute-start.10) | collective-permute-done | bytes 262176 | tf_op jit(solution)/shard_map/ppermute | solution.py:272
  216.1 1.1 collective-permute-start.11
  217.4 1.6 collective-permute-start.13
  218.9 2.7 %collective-permute-done.15 = bf16[2,32,2048]{2,1,0:T(8,128)(2,1)S(1)} collective-permute-done((bf16[2,32,2048]{2,1,0:T(8,128)(2,1)S(1)}, bf16[2,32,2048]{2,1,0:T(8,128)(2,1)S(1)}, u32[]{:S(2)}, u32[]{:S(2)}) %collective-permute-start.15) | collective-permute-done | bytes 262176 | tf_op jit(solution)/shard_map/ppermute | solution.py:272
  221.8 1.1 collective-permute-start.16
  223.0 1.6 collective-permute-start.18
  224.6 1.1 collective-permute-done.11
  225.8 1.5 collective-permute-done.16
  227.3 0.7 collective-permute-done.18
  228.1 0.9 fusion.12
  (106 shorter events, 8.0 us)
Async XLA Ops:
  7.2 35.1 %copy-start = (s32[4,2]{0,1:T(2,128)S(1)}, s32[4,2]{0,1:T(2,128)}, u32[]{:S(2)}) copy-start(s32[4,2]{0,1:T(2,128)} %param.19) | copy-start | bytes 100
  7.2 75.5 %reduce-scatter.2.cloned.1.call-start = ((), (), s32[]{:S(2)}) async-start(), calls=%async_computation.3 | async-start | bytes 2359296 | tf_op jit(solution)/shard_map/reduce_scatter | solution.py:353
  7.2 15.2 %collective-permute-start.3 = (bf16[32,8192]{1,0:T(8,128)(2,1)}, bf16[32,8192]{1,0:T(8,128)(2,1)S(1)}, u32[]{:S(2)}, u32[]{:S(2)}) collective-permute-start(bf16[32,8192]{1,0:T(8,128)(2,1)} %bitcast.92), channel_id=1, source_target_pairs={{0,4},{1,5},{2,6},{3,7},{4,0},{5,1},{6,2},{7,3},{8,12},{9,13},{10,... | collective-permute-start | bytes 1572872 | tf_op jit(solution)/shard_map/ppermute | solution.py:272
  10.3 13.9 %collective-permute-start.1 = (bf16[32,8192]{1,0:T(8,128)(2,1)}, bf16[32,8192]{1,0:T(8,128)(2,1)S(1)}, u32[]{:S(2)}, u32[]{:S(2)}) collective-permute-start(bf16[32,8192]{1,0:T(8,128)(2,1)} %bitcast.93), channel_id=1, source_target_pairs={{0,2},{1,3},{2,0},{3,1},{4,6},{5,7},{6,4},{7,5},{8,10},{9,11},{10,... | collective-permute-start | bytes 1572872 | tf_op jit(solution)/shard_map/ppermute | solution.py:272
  11.8 19.4 %collective-permute-start = (bf16[32,8192]{1,0:T(8,128)(2,1)}, bf16[32,8192]{1,0:T(8,128)(2,1)S(1)}, u32[]{:S(2)}, u32[]{:S(2)}) collective-permute-start(bf16[32,8192]{1,0:T(8,128)(2,1)} %bitcast.94), channel_id=1, source_target_pairs={{0,1},{1,0},{2,3},{3,2},{4,5},{5,4},{6,7},{7,6},{8,9},{9,8},{10,11... | collective-permute-start | bytes 1572872 | tf_op jit(solution)/shard_map/ppermute | solution.py:272
  22.4 7.6 %collective-permute-start.5 = (bf16[32,4096]{1,0:T(8,128)(2,1)S(1)}, bf16[32,4096]{1,0:T(8,128)(2,1)S(1)}, u32[]{:S(2)}, u32[]{:S(2)}) collective-permute-start(bf16[32,4096]{1,0:T(8,128)(2,1)S(1)} %slice.54), channel_id=1, source_target_pairs={{0,2},{1,3},{2,0},{3,1},{4,6},{5,7},{6,4},{7,5},{8,10},{9,11},{10,... | collective-permute-start | bytes 786440 | tf_op jit(solution)/shard_map/ppermute | solution.py:272
  24.2 7.0 %collective-permute-start.7 = (bf16[32,4096]{1,0:T(8,128)(2,1)S(1)}, bf16[32,4096]{1,0:T(8,128)(2,1)S(1)}, u32[]{:S(2)}, u32[]{:S(2)}) collective-permute-start(bf16[32,4096]{1,0:T(8,128)(2,1)S(1)} %slice.55), channel_id=1, source_target_pairs={{0,4},{1,5},{2,6},{3,7},{4,0},{5,1},{6,2},{7,3},{8,12},{9,13},{10,... | collective-permute-start | bytes 786440 | tf_op jit(solution)/shard_map/ppermute | solution.py:272
  25.8 7.0 %collective-permute-start.2 = (bf16[32,8192]{1,0:T(8,128)(2,1)S(1)}, bf16[32,8192]{1,0:T(8,128)(2,1)S(1)}, u32[]{:S(2)}, u32[]{:S(2)}) collective-permute-start(bf16[32,8192]{1,0:T(8,128)(2,1)S(1)} %collective-permute-done.1.refs_2_), channel_id=1, source_target_pairs={{0,1},{1,0},{2,3},{3,2},{4,5},{5,4},{6,7},{7,6},{8,9},{9,8},{10,11... | collective-permute-start | bytes 1572872 | tf_op jit(solution)/shard_map/ppermute | solution.py:272
  25.8 7.0 %collective-permute-start.4 = (bf16[32,8192]{1,0:T(8,128)(2,1)S(1)}, bf16[32,8192]{1,0:T(8,128)(2,1)S(1)}, u32[]{:S(2)}, u32[]{:S(2)}) collective-permute-start(bf16[32,8192]{1,0:T(8,128)(2,1)S(1)} %collective-permute-done.3.refs_4_), channel_id=1, source_target_pairs={{0,1},{1,0},{2,3},{3,2},{4,5},{5,4},{6,7},{7,6},{8,9},{9,8},{10,11... | collective-permute-start | bytes 1572872 | tf_op jit(solution)/shard_map/ppermute | solution.py:272
  30.0 1.5 collective-permute-start.6
  31.2 9.8 %copy-start.9 = (bf16[32,4096]{1,0:T(8,128)(2,1)}, bf16[32,4096]{1,0:T(8,128)(2,1)S(1)}, u32[]{:S(2)}) copy-start(bf16[32,4096]{1,0:T(8,128)(2,1)S(1)} %collective-permute-done.7.refs_8_) | copy-start | bytes 786436
  31.2 1.7 collective-permute-start.8
  31.5 9.5 %copy-start.11 = (bf16[32,4096]{1,0:T(8,128)(2,1)}, bf16[32,4096]{1,0:T(8,128)(2,1)S(1)}, u32[]{:S(2)}) copy-start(bf16[32,4096]{1,0:T(8,128)(2,1)S(1)} %collective-permute-done.6.refs_7_) | copy-start | bytes 786436
  32.9 2.2 copy-start.3
  35.0 1.0 copy-start.4
  41.0 0.7 copy-start.16
  41.0 52.1 %copy-start.14 = (s32[4,24]{1,0:T(4,128)S(1)}, s32[4,24]{1,0:T(4,128)}, u32[]{:S(2)}) copy-start(s32[4,24]{1,0:T(4,128)} %slot_ref.1) | copy-start | bytes 1156
  41.0 52.1 %copy-start.15 = (s32[4,24]{1,0:T(4,128)S(1)}, s32[4,24]{1,0:T(4,128)}, u32[]{:S(2)}) copy-start(s32[4,24]{1,0:T(4,128)} %holder_ref.3) | copy-start | bytes 1156
  84.7 1.8 copy-start.20
  88.5 15.2 %all-to-all-start.1 = ((bf16[32,16,256]{2,1,0:T(8,128)(2,1)}), bf16[32,16,256]{2,1,0:T(8,128)(2,1)S(1)}, u32[]{:S(2)}, u32[]{:S(2)}) async-start(bf16[32,16,256]{2,1,0:T(8,128)(2,1)} %bitcast_select_fusion), calls=%async_computation.2 | async-start | bytes 524288 | tf_op jit(solution)/shard_map/all_to_all | solution.py:406
  93.1 1.4 copy-start.6
  103.7 0.7 copy-start.17
  104.4 3.9 %copy-start.5 = (bf16[1,32,8192]{2,1,0:T(8,128)(2,1)S(1)}, bf16[1,32,8192]{2,1,0:T(8,128)(2,1)}, u32[]{:S(2)}) copy-start(bf16[1,32,8192]{2,1,0:T(8,128)(2,1)} %param.10) | copy-start | bytes 1572868
  104.4 75.3 %all-to-all-start = ((bf16[32,192,256]{2,1,0:T(8,128)(2,1)}), bf16[32,192,256]{2,1,0:T(8,128)(2,1)}, u32[]{:S(2)}, u32[]{:S(2)}) async-start(bf16[32,192,256]{2,1,0:T(8,128)(2,1)} %bitcast.4), calls=%async_computation | async-start | bytes 6291456 | tf_op jit(solution)/shard_map/all_to_all | solution.py:337
  108.3 5.8 %copy-start.2 = (bf16[8192,1024]{1,0:T(8,128)(2,1)S(1)}, bf16[8192,1024]{1,0:T(8,128)(2,1)}, u32[]{:S(2)}) copy-start(bf16[8192,1024]{1,0:T(8,128)(2,1)} %refs_10_.2) | copy-start | bytes 50331652
  114.1 0.9 copy-start.10
  115.1 0.9 copy-start.12
  116.0 8.8 %copy-start.19 = (bf16[256,128]{1,0:T(8,128)(2,1)S(1)}, bf16[256,128]{1,0:T(8,128)(2,1)}, u32[]{:S(2)}) copy-start(bf16[256,128]{1,0:T(8,128)(2,1)} %copy-done.18) | copy-start | bytes 196612
  116.0 8.8 %copy-start.21 = (bf16[256,128]{1,0:T(8,128)(2,1)S(1)}, bf16[256,128]{1,0:T(8,128)(2,1)}, u32[]{:S(2)}) copy-start(bf16[256,128]{1,0:T(8,128)(2,1)} %copy-done.20) | copy-start | bytes 196612
  123.8 1.0 copy-start.7
  179.7 1.2 copy-start.8
  180.9 0.9 copy-start.13
  181.8 21.5 %slice-start = ((s8[16777216]{0:T(1024)(128)(4,1)}), s8[4194304]{0:T(1024)(128)(4,1)S(1)}, s32[]{:S(2)}) async-start(s8[16777216]{0:T(1024)(128)(4,1)} %bitcast.107), calls=%async_computation.4 | async-start | bytes 8388608
  181.8 21.5 %slice-start.1 = ((s8[16777216]{0:T(1024)(128)(4,1)}), s8[4194304]{0:T(1024)(128)(4,1)S(1)}, s32[]{:S(2)}) async-start(s8[16777216]{0:T(1024)(128)(4,1)} %bitcast.107), calls=%async_computation.5 | async-start | bytes 8388608
  197.2 6.1 %slice-start.2 = ((s8[16777216]{0:T(1024)(128)(4,1)}), s8[4194304]{0:T(1024)(128)(4,1)S(1)}, s32[]{:S(2)}) async-start(s8[16777216]{0:T(1024)(128)(4,1)} %bitcast.107), calls=%async_computation.6 | async-start | bytes 8388608
  197.3 6.1 %slice-start.3 = ((s8[16777216]{0:T(1024)(128)(4,1)}), s8[4194304]{0:T(1024)(128)(4,1)S(1)}, s32[]{:S(2)}) async-start(s8[16777216]{0:T(1024)(128)(4,1)} %bitcast.107), calls=%async_computation.7 | async-start | bytes 8388608
  203.2 3.2 %collective-permute-start.9 = (bf16[2,2,32,4096]{3,2,1,0:T(8,128)(2,1)S(1)}, bf16[2,2,32,4096]{3,2,1,0:T(8,128)(2,1)S(1)}, u32[]{:S(2)}, u32[]{:S(2)}) collective-permute-start(bf16[2,2,32,4096]{3,2,1,0:T(8,128)(2,1)S(1)} %dynamic-slice_bitcast_fusion.1), channel_id=1, source_target_pairs={{0,1},{1,0},{2,3},{3,2},{4,5},{5,4},{6,7},{7,6},{8,9},{9,8},{10,11... | collective-permute-start | bytes 3145736 | tf_op jit(solution)/shard_map/ppermute | solution.py:272
  205.9 3.7 %collective-permute-start.14 = (bf16[2,2,32,4096]{3,2,1,0:T(8,128)(2,1)S(1)}, bf16[2,2,32,4096]{3,2,1,0:T(8,128)(2,1)S(1)}, u32[]{:S(2)}, u32[]{:S(2)}) collective-permute-start(bf16[2,2,32,4096]{3,2,1,0:T(8,128)(2,1)S(1)} %dynamic-slice_bitcast_fusion), channel_id=1, source_target_pairs={{0,1},{1,0},{2,3},{3,2},{4,5},{5,4},{6,7},{7,6},{8,9},{9,8},{10,11... | collective-permute-start | bytes 3145736 | tf_op jit(solution)/shard_map/ppermute | solution.py:272
  206.8 9.2 %collective-permute-start.10 = (bf16[2,32,2048]{2,1,0:T(8,128)(2,1)S(1)}, bf16[2,32,2048]{2,1,0:T(8,128)(2,1)S(1)}, u32[]{:S(2)}, u32[]{:S(2)}) collective-permute-start(bf16[2,32,2048]{2,1,0:T(8,128)(2,1)S(1)} %dynamic-slice_bitcast_fusion.5), channel_id=1, source_target_pairs={{0,2},{1,3},{2,0},{3,1},{4,6},{5,7},{6,4},{7,5},{8,10},{9,11},{10,... | collective-permute-start | bytes 786440 | tf_op jit(solution)/shard_map/ppermute | solution.py:272
  208.0 9.3 %collective-permute-start.12 = (bf16[2,32,2048]{2,1,0:T(8,128)(2,1)S(1)}, bf16[2,32,2048]{2,1,0:T(8,128)(2,1)S(1)}, u32[]{:S(2)}, u32[]{:S(2)}) collective-permute-start(bf16[2,32,2048]{2,1,0:T(8,128)(2,1)S(1)} %dynamic-slice_bitcast_fusion.4), channel_id=1, source_target_pairs={{0,4},{1,5},{2,6},{3,7},{4,0},{5,1},{6,2},{7,3},{8,12},{9,13},{10,... | collective-permute-start | bytes 786440 | tf_op jit(solution)/shard_map/ppermute | solution.py:272
  209.9 11.7 %collective-permute-start.15 = (bf16[2,32,2048]{2,1,0:T(8,128)(2,1)S(1)}, bf16[2,32,2048]{2,1,0:T(8,128)(2,1)S(1)}, u32[]{:S(2)}, u32[]{:S(2)}) collective-permute-start(bf16[2,32,2048]{2,1,0:T(8,128)(2,1)S(1)} %dynamic-slice_bitcast_fusion.3), channel_id=1, source_target_pairs={{0,2},{1,3},{2,0},{3,1},{4,6},{5,7},{6,4},{7,5},{8,10},{9,11},{10,... | collective-permute-start | bytes 786440 | tf_op jit(solution)/shard_map/ppermute | solution.py:272
  210.5 12.4 %collective-permute-start.17 = (bf16[2,32,2048]{2,1,0:T(8,128)(2,1)S(1)}, bf16[2,32,2048]{2,1,0:T(8,128)(2,1)S(1)}, u32[]{:S(2)}, u32[]{:S(2)}) collective-permute-start(bf16[2,32,2048]{2,1,0:T(8,128)(2,1)S(1)} %dynamic-slice_bitcast_fusion.2), channel_id=1, source_target_pairs={{0,4},{1,5},{2,6},{3,7},{4,0},{5,1},{6,2},{7,3},{8,12},{9,13},{10,... | collective-permute-start | bytes 786440 | tf_op jit(solution)/shard_map/ppermute | solution.py:272
  216.1 9.6 %collective-permute-start.11 = (bf16[32,2048]{1,0:T(8,128)(2,1)S(1)}, bf16[32,2048]{1,0:T(8,128)(2,1)S(1)}, u32[]{:S(2)}, u32[]{:S(2)}) collective-permute-start(bf16[32,2048]{1,0:T(8,128)(2,1)S(1)} %fusion.17), channel_id=1, source_target_pairs={{0,4},{1,5},{2,6},{3,7},{4,0},{5,1},{6,2},{7,3},{8,12},{9,13},{10,... | collective-permute-start | bytes 393224 | tf_op jit(solution)/shard_map/ppermute | solution.py:272
  217.4 8.4 %collective-permute-start.13 = (bf16[32,2048]{1,0:T(8,128)(2,1)S(1)}, bf16[32,2048]{1,0:T(8,128)(2,1)S(1)}, u32[]{:S(2)}, u32[]{:S(2)}) collective-permute-start(bf16[32,2048]{1,0:T(8,128)(2,1)S(1)} %fusion.18), channel_id=1, source_target_pairs={{0,2},{1,3},{2,0},{3,1},{4,6},{5,7},{6,4},{7,5},{8,10},{9,11},{10,... | collective-permute-start | bytes 393224 | tf_op jit(solution)/shard_map/ppermute | solution.py:272
  221.7 6.3 %copy-start.22 = (bf16[1,32,8192]{2,1,0:T(8,128)(2,1)S(1)}, bf16[1,32,8192]{2,1,0:T(8,128)(2,1)}, u32[]{:S(2)}) copy-start(bf16[1,32,8192]{2,1,0:T(8,128)(2,1)} %param.11) | copy-start | bytes 1572868
  221.8 5.5 %collective-permute-start.16 = (bf16[32,2048]{1,0:T(8,128)(2,1)S(1)}, bf16[32,2048]{1,0:T(8,128)(2,1)S(1)}, u32[]{:S(2)}, u32[]{:S(2)}) collective-permute-start(bf16[32,2048]{1,0:T(8,128)(2,1)S(1)} %fusion.19), channel_id=1, source_target_pairs={{0,4},{1,5},{2,6},{3,7},{4,0},{5,1},{6,2},{7,3},{8,12},{9,13},{10,... | collective-permute-start | bytes 393224 | tf_op jit(solution)/shard_map/ppermute | solution.py:272
  223.0 5.0 %collective-permute-start.18 = (bf16[32,2048]{1,0:T(8,128)(2,1)S(1)}, bf16[32,2048]{1,0:T(8,128)(2,1)S(1)}, u32[]{:S(2)}, u32[]{:S(2)}) collective-permute-start(bf16[32,2048]{1,0:T(8,128)(2,1)S(1)} %fusion.20), channel_id=1, source_target_pairs={{0,2},{1,3},{2,0},{3,1},{4,6},{5,7},{6,4},{7,5},{8,10},{9,11},{10,... | collective-permute-start | bytes 393224 | tf_op jit(solution)/shard_map/ppermute | solution.py:272
  225.7 3.3 %copy-start.1 = (s32[4,2]{0,1:T(2,128)S(1)}, s32[4,2]{0,1:T(2,128)}, u32[]{:S(2)}) copy-start(s32[4,2]{0,1:T(2,128)} %param.19) | copy-start | bytes 100
  (1 other events, 0.6 us)
Sparse Core Ops, SparseCore 0:
  41.1 41.5 reduce-scatter.1

commit v3 on v2

v3 whole, which is shorter than its diff:
```python
import functools
import math

import jax
import jax.numpy as jnp
from jax import lax
from jax.experimental import pallas as pl
from jax.experimental.pallas import tpu as pltpu
from jax.sharding import PartitionSpec as P

KVH = 8
HD = 128
BLK = 128
LOG2E = 1.4426950408889634


def frequencies(width):
    half_width = width // 2
    base_freq = jnp.power(
        jnp.float32(500000.0), -jnp.arange(half_width, dtype=jnp.float32) * (2.0 / width)
    )
    wavelength = 2.0 * math.pi / base_freq
    blended = (8192.0 / wavelength - 1.0) / 3.0
    middle = (1.0 - blended) * base_freq / 8.0 + blended * base_freq
    return jnp.where(
        wavelength < 2048.0, base_freq, jnp.where(wavelength > 8192.0, base_freq / 8.0, middle)
    )


def rope_tables(positions):
    angles = positions.astype(jnp.float32)[:, None] * frequencies(HD)[None, :]
    cosine, sine = jnp.cos(angles), jnp.sin(angles)
    return jnp.concatenate([cosine, cosine], axis=1), jnp.concatenate([-sine, sine], axis=1)


def split_kernel(pool_ref, hidden_ref, out_ref):
    key_width = KVH * HD
    slots, block_rows, _ = pool_ref.shape
    width = out_ref.shape[3]

    def one(slot, carry):
        rows = pool_ref[slot]
        for head in range(KVH):
            at = head * HD
            out_ref[head, slot] = jnp.concatenate(
                [rows[:, at : at + HD], rows[:, key_width + at : key_width + at + HD]], axis=1
            )
        return carry

    lax.fori_loop(0, slots, one, 0)
    rows, features = hidden_ref.shape
    share = features // KVH
    for dest in range(KVH):
        for chunk in range(share // width):
            at = dest * share + chunk * width
            for r in range(rows // block_rows):
                out_ref[dest, slots + chunk * (rows // block_rows) + r] = hidden_ref[
                    r * block_rows : (r + 1) * block_rows, at : at + width
                ]


def split_heads(kv_pool, own):
    slots, block_rows, _ = kv_pool.shape
    extra = own.size // (KVH * block_rows * 2 * HD)
    shape = (KVH, slots + extra, block_rows, 2 * HD)
    return pl.pallas_call(
        split_kernel,
        grid=(1,),
        in_specs=[
            pl.BlockSpec(kv_pool.shape, lambda i: (0, 0, 0)),
            pl.BlockSpec(own.shape, lambda i: (0, 0)),
        ],
        out_specs=pl.BlockSpec(shape, lambda i: (0, 0, 0, 0)),
        out_shape=jax.ShapeDtypeStruct(shape, kv_pool.dtype),
        compiler_params=pltpu.CompilerParams(vmem_limit_bytes=16 * 1024 * 1024),
    )(kv_pool, own)


def pack_kernel(group_ref, holder_ref, slot_ref, pool_ref, *out_refs):
    ranks, _, block_rows, _ = pool_ref.shape
    group = group_ref[0]
    main_ref = out_refs[0]
    cap = main_ref.shape[1]
    for distance, more_ref in enumerate(out_refs[1:], start=1):
        request = group ^ distance

        def one(index, count, more_ref=more_ref, request=request):
            mine = holder_ref[request, index] == group
            slot = slot_ref[request, index]

            @pl.when(mine & (count < cap))
            def _():
                for r in range(ranks):
                    rows = slice(r * block_rows, (r + 1) * block_rows)
                    main_ref[request, count, rows, :] = pool_ref[r, slot]

            @pl.when(mine & (count >= cap))
            def _():
                for r in range(ranks):
                    rows = slice(r * block_rows, (r + 1) * block_rows)
                    more_ref[count - cap, rows, :] = pool_ref[r, slot]

            return count + mine.astype(jnp.int32)

        lax.fori_loop(0, holder_ref.shape[1], one, jnp.int32(0))


def pack(group, hit_holder, hit_slot, pool, cap, base):
    ranks, slots, block_rows, width = pool.shape
    block = (ranks * block_rows, width)
    shapes = [(hit_holder.shape[0], base, *block)] + [(cap - base, *block)] * 3
    return pl.pallas_call(
        pack_kernel,
        grid_spec=pltpu.PrefetchScalarGridSpec(
            num_scalar_prefetch=3,
            grid=(1,),
            in_specs=[pl.BlockSpec(pool.shape, lambda i, *_: (0, 0, 0, 0))],
            out_specs=[
                pl.BlockSpec(shape, lambda i, *_, n=len(shape): (0,) * n) for shape in shapes
            ],
        ),
        out_shape=[jax.ShapeDtypeStruct(shape, pool.dtype) for shape in shapes],
        compiler_params=pltpu.CompilerParams(vmem_limit_bytes=24 * 1024 * 1024),
    )(group, hit_holder, hit_slot, pool)


def place_pieces(group, length, holder_ref, slot_ref, refs, prefix_ref):
    pool_ref, main_ref, near_ref, two_ref, three_ref = refs
    ranks, _, block_rows, _ = pool_ref.shape
    rows = ranks * block_rows
    base = main_ref.shape[1]

    def one(index, counts):
        holder = holder_ref[group, index]
        distance = holder ^ group
        count = sum(jnp.where(distance == d, counts[d], 0) for d in range(4))
        at = pl.multiple_of(index * rows, rows)
        seen = index * rows < length

        @pl.when(jnp.logical_not(seen))
        def _():
            prefix_ref[pl.ds(at, rows), :] = jnp.zeros((rows, 2 * HD), jnp.bfloat16)

        @pl.when(seen & (distance == 0))
        def _():
            slot = slot_ref[group, index]
            for r in range(ranks):
                prefix_ref[pl.ds(at + r * block_rows, block_rows), :] = pool_ref[r, slot]

        low = count < base
        rest = count - base

        @pl.when(seen & (distance != 0) & low)
        def _():
            prefix_ref[pl.ds(at, rows), :] = main_ref[holder, count]

        def take(when, ref, n):
            @pl.when(seen & when)
            def _():
                prefix_ref[pl.ds(at, rows), :] = ref[n]

        take((distance == 1) & ~low, near_ref, rest)
        take((distance == 2) & ~low, two_ref, rest)
        take((distance == 3) & ~low, three_ref, rest)
        return tuple(n + (distance == d).astype(jnp.int32) for d, n in enumerate(counts))

    lax.fori_loop(0, holder_ref.shape[1], one, (jnp.int32(0),) * 4)


def attention_kernel(
    tile, ordered, length_ref, group_ref, holder_ref, slot_ref, q_ref, cos_ref, sin_ref, summed_ref, *refs
):
    *piece_refs, out_ref, fresh_ref, prefix_ref = refs
    group = group_ref[0]
    span = prefix_ref.shape[0]
    row0 = pl.program_id(1) * tile

    @pl.when((pl.program_id(0) == 0) & (pl.program_id(1) == 0))
    def _():
        if ordered:
            prefix_ref[...] = piece_refs[0][...]
        else:
            place_pieces(group, length_ref[group], holder_ref, slot_ref, piece_refs, prefix_ref)
        keys = summed_ref[:, :HD]
        keys = keys * cos_ref[...] + pltpu.roll(keys, HD // 2, 1) * sin_ref[...]
        fresh_ref[:, :HD] = keys.astype(jnp.bfloat16)
        fresh_ref[:, HD:] = summed_ref[:, HD:].astype(jnp.bfloat16)

    seen = lax.broadcasted_iota(jnp.int32, (1, span), 1) < length_ref[group]
    bias = jnp.where(seen, 0.0, -1e30)
    columns = lax.broadcasted_iota(jnp.int32, (tile, fresh_ref.shape[0]), 1)
    rows = lax.broadcasted_iota(jnp.int32, (tile, fresh_ref.shape[0]), 0) + row0
    causal = columns <= rows
    cosine = cos_ref[pl.ds(pl.multiple_of(row0, tile), tile), :]
    sine = sin_ref[pl.ds(pl.multiple_of(row0, tile), tile), :]
    factor = HD ** (-0.5) * LOG2E

    def scores(query, keys):
        return lax.dot_general(
            query, keys, (((1,), (1,)), ((), ())), preferred_element_type=jnp.float32
        )

    for head in range(q_ref.shape[1] // HD):
        lanes = slice(head * HD, (head + 1) * HD)
        raw = q_ref[:, lanes]
        query = raw * cosine + pltpu.roll(raw, HD // 2, 1) * sine
        query = (query * factor).astype(jnp.bfloat16)
        old = scores(query, prefix_ref[:, :HD]) + bias
        new = jnp.where(causal, scores(query, fresh_ref[:, :HD]), -1e30)
        peak = jnp.maximum(
            jnp.max(old, axis=1, keepdims=True), jnp.max(new, axis=1, keepdims=True)
        )
        old, new = jnp.exp2(old - peak), jnp.exp2(new - peak)
        total = jnp.sum(old, axis=1, keepdims=True) + jnp.sum(new, axis=1, keepdims=True)
        mixed = jnp.dot(
            old.astype(jnp.bfloat16), prefix_ref[:, HD:], preferred_element_type=jnp.float32
        ) + jnp.dot(
            new.astype(jnp.bfloat16), fresh_ref[:, HD:], preferred_element_type=jnp.float32
        )
        out_ref[:, lanes] = (mixed / total).astype(jnp.bfloat16)


def attention(
    prefix_len, group, hit_holder, hit_slot, raw_queries, cosine, sine, summed, pieces, ordered
):
    rows, width = raw_queries.shape
    tile = min(256, rows)
    span = hit_holder.shape[1] * BLK
    keys = span + rows

    def whole(array):
        return pl.BlockSpec(array.shape, lambda h, t, *_: (0,) * array.ndim)

    return pl.pallas_call(
        functools.partial(attention_kernel, tile, ordered),
        grid_spec=pltpu.PrefetchScalarGridSpec(
            num_scalar_prefetch=4,
            grid=(width // (2 * HD), rows // tile),
            in_specs=[
                pl.BlockSpec((tile, 2 * HD), lambda h, t, *_: (t, h)),
                whole(cosine),
                whole(sine),
                whole(summed),
            ]
            + [whole(piece) for piece in pieces],
            out_specs=[pl.BlockSpec((tile, 2 * HD), lambda h, t, *_: (t, h)), whole(summed)],
            scratch_shapes=[pltpu.VMEM((span, 2 * HD), jnp.bfloat16)],
        ),
        out_shape=[
            jax.ShapeDtypeStruct((rows, width), jnp.bfloat16),
            jax.ShapeDtypeStruct(summed.shape, jnp.bfloat16),
        ],
        compiler_params=pltpu.CompilerParams(vmem_limit_bytes=40 * 1024 * 1024),
        cost_estimate=pl.CostEstimate(
            flops=4 * rows * width * keys,
            bytes_accessed=rows * width * 6,
            transcendentals=rows * width // HD * keys,
        ),
    )(prefix_len, group, hit_holder, hit_slot, raw_queries, cosine, sine, summed, *pieces)


PAIRS = ((0, 2), (1, 3), (0, 3), (1, 2))


def pairs_wanted(prefix_len, hit_holder, base):
    requests, blocks = hit_holder.shape
    starts = jnp.arange(blocks, dtype=jnp.int32) * BLK
    seen = starts[None, :] < prefix_len[:, None]
    holders = jnp.arange(requests, dtype=jnp.int32)
    held = (hit_holder[:, None, :] == holders[None, :, None]) & seen[:, None, :]
    over = jnp.sum(held.astype(jnp.int32), axis=2) > base
    bits = [[0] * requests for _ in range(requests)]
    for n, (one, other) in enumerate(PAIRS):
        bits[one][other] = bits[other][one] = n + 1
    numbers = jnp.asarray(bits, jnp.int32)
    flags = [jnp.any(over & (numbers == n + 1)) for n in range(len(PAIRS))]
    return sum(flag.astype(jnp.int32) << n for n, flag in enumerate(flags))


def exchange_more(more, wanted):
    def branch(bits):
        def run(two, three):
            out = []
            for array, at in ((two, 0), (three, 2)):
                pairs = [PAIRS[n] for n in (at, at + 1) if bits >> n & 1]
                moves = [pair for one, other in pairs for pair in ((one, other), (other, one))]
                out.append(lax.ppermute(array, "req", moves) if moves else array)
            return tuple(out)

        return run

    return list(lax.switch(wanted, [branch(bits) for bits in range(16)], *more))


def keyval_kernel(slots, rows, mixed_ref, weight_ref, out_ref):
    ranks, groups, block_rows, width = mixed_ref.shape
    tall = rows // block_rows
    tokens = jnp.concatenate(
        [
            jnp.concatenate(
                [
                    mixed_ref[r, at + i]
                    for at in range(slots, groups, tall)
                ],
                axis=1,
            )
            for r in range(ranks)
            for i in range(tall)
        ],
        axis=0,
    )
    key_width = KVH * HD
    product = jnp.dot(tokens, weight_ref[...], preferred_element_type=jnp.float32)
    for head in range(KVH):
        at = head * HD
        out_ref[head, :, :HD] = product[:, at : at + HD]
        out_ref[head, :, HD:] = product[:, key_width + at : key_width + at + HD]


def keyval_project(mixed, slots, rows, w_keyval):
    depth, width = w_keyval.shape
    count = mixed.shape[0] * rows
    shape = (KVH, count, 2 * HD)
    return pl.pallas_call(
        functools.partial(keyval_kernel, slots, rows),
        grid=(1,),
        in_specs=[
            pl.BlockSpec(mixed.shape, lambda i: (0, 0, 0, 0)),
            pl.BlockSpec((depth, width), lambda i: (0, 0)),
        ],
        out_specs=pl.BlockSpec(shape, lambda i: (0, 0, 0)),
        out_shape=jax.ShapeDtypeStruct(shape, jnp.float32),
        compiler_params=pltpu.CompilerParams(vmem_limit_bytes=24 * 1024 * 1024),
        cost_estimate=pl.CostEstimate(flops=1024, bytes_accessed=1024, transcendentals=0),
    )(mixed, w_keyval)


def query_kernel(rank_ref, *refs):
    parts, weight_ref, out_ref, tokens_ref = refs[:10], refs[10], refs[11], refs[12]
    rank = rank_ref[0]
    rows, half = parts[6].shape

    @pl.when(pl.program_id(0) == 0)
    def _():
        for b in range(8):
            to = pl.multiple_of((rank ^ b) * rows, rows)
            if b < 6:
                tokens_ref[pl.ds(to, rows), :] = parts[b][...]
            else:
                tokens_ref[pl.ds(to, rows), :half] = parts[b][...]
                tokens_ref[pl.ds(to, rows), half:] = parts[b + 2][...]

    out_ref[...] = jnp.dot(tokens_ref[...], weight_ref[...], preferred_element_type=jnp.float32)


def query_project(rank, parts, w_query):
    rows, depth = parts[0].shape
    width = w_query.shape[1]
    block = 256
    return pl.pallas_call(
        query_kernel,
        grid_spec=pltpu.PrefetchScalarGridSpec(
            num_scalar_prefetch=1,
            grid=(width // block,),
            in_specs=[pl.BlockSpec(part.shape, lambda i, r: (0, 0)) for part in parts]
            + [pl.BlockSpec((depth, block), lambda i, r: (0, i))],
            out_specs=pl.BlockSpec((8 * rows, block), lambda i, r: (0, i)),
            scratch_shapes=[pltpu.VMEM((8 * rows, depth), jnp.bfloat16)],
        ),
        out_shape=jax.ShapeDtypeStruct((8 * rows, width), jnp.float32),
        compiler_params=pltpu.CompilerParams(vmem_limit_bytes=50 * 1024 * 1024),
        cost_estimate=pl.CostEstimate(flops=1024, bytes_accessed=1024, transcendentals=0),
    )(rank, *parts, w_query)


def gather_parts(own):
    half = own.shape[1] // 2
    near_x, near_y, near_core = swap(own, 2, 8), swap(own, 4, 8), swap(own, 1, 8)
    left = swap(near_y[:, :half], 2, 8)
    right = swap(near_x[:, half:], 4, 8)
    return [
        own, near_core, near_x, swap(near_x, 1, 8), near_y, swap(near_y, 1, 8),
        left, swap(left, 1, 8), right, swap(right, 1, 8),
    ]


def swap(array, bit, count):
    return lax.ppermute(array, "cp", [(i, i ^ bit) for i in range(count)])


def pick(array, index, axis):
    return lax.dynamic_index_in_dim(array, index, axis, keepdims=False)


def add(one, two):
    return one.astype(jnp.float32) + two.astype(jnp.float32)


def scatter_sum(part, rank):
    rows, width = part.shape
    core, x, y = rank % 2, rank // 2 % 2, rank // 4
    view = part.reshape(2, 2, 2, rows // 8, width)
    got = swap(pick(view, 1 - core, 2), 1, 8)
    pair = add(pick(view, core, 2), got).astype(jnp.bfloat16)
    half = width // 2
    one, two = pair[..., :half], pair[..., half:]
    got_one = swap(pick(one, 1 - x, 1), 2, 8)
    got_two = swap(pick(two, 1 - y, 0), 4, 8)
    one = add(pick(one, x, 1), got_one)
    two = add(pick(two, y, 0), got_two)
    end_one = swap(pick(one, 1 - y, 0).astype(jnp.bfloat16), 4, 8)
    end_two = swap(pick(two, 1 - x, 0).astype(jnp.bfloat16), 2, 8)
    one = add(pick(one, y, 0), end_one)
    two = add(pick(two, x, 0), end_two)
    return jnp.concatenate([one, two], axis=1)


def local(
    hidden, residual, w_query, w_keyval, w_out, kv_pool, prefix_len, hit_holder, hit_slot, owner
):
    cp_count = lax.axis_size("cp")
    group_id = lax.axis_index("req")
    cp_rank = lax.axis_index("cp")
    tok_rows = hidden.shape[1]
    stretch_rows = tok_rows * cp_count
    slice_rows = w_keyval.shape[0]
    block_rows = kv_pool.shape[1]
    request_count = hit_holder.shape[0]
    prefix_blocks = hit_holder.shape[1]
    new_blocks = owner.shape[1]
    owner_cap = (new_blocks + 1) // 2
    holder_cap = prefix_blocks // 2
    heads_share = cp_count // KVH
    length = prefix_len[group_id]
    positions = length + jnp.arange(stretch_rows, dtype=jnp.int32)
    cosine, sine = rope_tables(positions)

    group = group_id.reshape(1)
    rank = cp_rank.reshape(1)
    fast = cp_count == 8 and request_count == 4 and block_rows % 16 == 0
    own = hidden[0]
    if fast:
        pool = lax.all_to_all(
            split_heads(kv_pool, own), "cp", split_axis=0, concat_axis=0, tiled=True
        )
        base = holder_cap // 2
        wanted = pairs_wanted(prefix_len, hit_holder, base)
        pool, cosine, sine, wanted = lax.optimization_barrier((pool, cosine, sine, wanted))
        packed = pack(group, hit_holder, hit_slot, pool, holder_cap, base)
        own, pool, packed = lax.optimization_barrier((own, pool, packed))
        main, near, two_more, three_more = packed
        main = lax.all_to_all(main, "req", split_axis=0, concat_axis=0, tiled=True)
        near = lax.ppermute(near, "req", [(i, i ^ 1) for i in range(4)])
        partial_kv = keyval_project(pool, kv_pool.shape[0], tok_rows, w_keyval)
        summed = lax.psum_scatter(partial_kv, "cp", scatter_dimension=0, tiled=True)[0]
        raw_queries = query_project(rank, gather_parts(own), w_query)
        more, raw_queries = lax.optimization_barrier(((two_more, three_more), raw_queries))
        pieces = [pool, main, near] + exchange_more(more, wanted)
    else:
        slot_ids = jnp.arange(holder_cap, dtype=jnp.int32)
        holds_hit = hit_holder == group_id
        hit_order = jnp.cumsum(holds_hit.astype(jnp.int32), axis=1) - 1
        picked = holds_hit[:, None, :] & (hit_order[:, None, :] == slot_ids[None, :, None])
        sources = jnp.sum(jnp.where(picked, hit_slot[:, None, :], 0), axis=2)
        by_head = kv_pool.reshape(-1, block_rows, 2, KVH, HD)[sources]
        by_head = jnp.transpose(by_head, (0, 4, 1, 2, 3, 5))
        sending = jnp.repeat(by_head, heads_share, axis=1).reshape(
            request_count * cp_count, holder_cap * block_rows, 2 * HD
        )
        arrived = lax.all_to_all(sending, ("req", "cp"), split_axis=0, concat_axis=0, tiled=True)
        arrived = arrived.reshape(request_count, cp_count, holder_cap, block_rows, 2 * HD)
        my_holders = hit_holder[group_id]
        hit_index = jnp.arange(prefix_blocks, dtype=jnp.int32)
        earlier = (my_holders[:, None] == my_holders[None, :]) & (
            hit_index[:, None] > hit_index[None, :]
        )
        hit_rank = jnp.sum(earlier.astype(jnp.int32), axis=1)
        pieces = [arrived[my_holders, :, hit_rank].reshape(prefix_blocks * BLK, 2 * HD)]

        gathered = lax.all_gather(own, "cp", axis=0, tiled=True)
        raw_queries = jnp.dot(gathered, w_query, preferred_element_type=jnp.float32)
        columns = lax.dynamic_slice_in_dim(gathered, cp_rank * slice_rows, slice_rows, 1)
        partial_kv = jnp.dot(columns, w_keyval, preferred_element_type=jnp.float32)
        partial_kv = jnp.transpose(
            partial_kv.reshape(stretch_rows, 2, KVH, HD), (2, 0, 1, 3)
        ).reshape(KVH, stretch_rows, 2 * HD)
        partial_kv = jnp.repeat(partial_kv, heads_share, axis=0)
        summed = lax.psum_scatter(partial_kv, "cp", scatter_dimension=0, tiled=True)[0]
    attended, fresh = attention(
        prefix_len, group, hit_holder, hit_slot, raw_queries, cosine, sine, summed, pieces, not fast
    )

    if fast:
        wide = w_out.shape[1] // 2
        sums = [
            scatter_sum(
                jnp.dot(
                    attended, w_out[:, at : at + wide], preferred_element_type=jnp.float32
                ).astype(jnp.bfloat16),
                cp_rank,
            )
            for at in range(0, w_out.shape[1], wide)
        ]
        projected = jnp.concatenate(sums, axis=1)
    else:
        projected = lax.psum_scatter(
            jnp.dot(attended, w_out, preferred_element_type=jnp.float32).astype(jnp.bfloat16),
            "cp",
            scatter_dimension=0,
            tiled=True,
        ).astype(jnp.float32)
    layer_out = (residual[0].astype(jnp.float32) + projected).astype(jnp.bfloat16)[None]

    my_owners = owner[group_id]
    block_ids = jnp.arange(new_blocks, dtype=jnp.int32)
    before = (my_owners[:, None] == my_owners[None, :]) & (block_ids[:, None] > block_ids[None, :])
    owner_rank = jnp.sum(before.astype(jnp.int32), axis=1)
    targets = jnp.arange(request_count, dtype=jnp.int32)[:, None, None]
    cap_ids = jnp.arange(owner_cap, dtype=jnp.int32)[None, :, None]
    chosen = (my_owners[None, None, :] == targets) & (owner_rank[None, None, :] == cap_ids)
    block_pick = jnp.sum(jnp.where(chosen, block_ids[None, None, :], 0), axis=2)
    present = jnp.any(chosen, axis=2)
    blocks = fresh.reshape(new_blocks, cp_count, block_rows, 2 * HD)[block_pick]
    blocks = jnp.where(present[:, :, None, None, None], blocks, jnp.zeros((), jnp.bfloat16))
    blocks = jnp.transpose(blocks, (0, 2, 1, 3, 4)).reshape(
        request_count * cp_count, owner_cap * block_rows, 2 * HD
    )
    blocks, _ = lax.optimization_barrier((blocks, attended))
    landed = lax.all_to_all(blocks, ("req", "cp"), split_axis=0, concat_axis=0, tiled=True)
    landed = landed.reshape(request_count, cp_count, owner_cap, block_rows, 2, HD)[:, ::heads_share]
    new_cache = jnp.transpose(landed, (0, 2, 3, 4, 1, 5)).reshape(
        1, request_count * owner_cap, block_rows, 2 * KVH * HD
    )
    return (layer_out, new_cache)


def solution(mesh):
    in_specs = (
        P("req", "cp", None),
        P("req", "cp", None),
        P(None, "cp"),
        P("cp", None),
        P("cp", None),
        P("req", "cp", None),
        P(),
        P(),
        P(),
        P(),
    )
    out_specs = (P("req", "cp", None), P("req", None, "cp", None))
    return jax.shard_map(local, mesh=mesh, in_specs=in_specs, out_specs=out_specs, check_vma=False)
```

time: 237 us -> 189 us (0.80)
  waiting for transfers between devices: 124 us -> 51.4 us
  starting transfers between devices: 27.5 us -> 42.7 us
  other arithmetic: 5.89 us -> 10.5 us
  matrix products: 8.28 us -> 11.7 us
  between operations: 14.6 us -> 17.1 us
    reduce_scatter x1, waiting for transfers between devices: 38.5 us -> 0.01 us  [local(): lax.psum_scatter(partial_kv, 'cp', scatter_dimension=0, tiled=True)[0]]
    all_to_all x1 -> x2, waiting for transfers between devices: 52.8 us -> 20.5 us  [the longest x1 20.5 us: local(): lax.all_to_all(split_heads(kv_pool, own), 'cp', split_axis=0, concat_axis...]
    all_to_all x1, starting transfers between devices: 4.61 us -> 15.1 us  [local(): lax.all_to_all(blocks, ('req', 'cp'), split_axis=0, concat_axis=0, tiled=...]
    all_to_all x1 -> x2, starting transfers between devices: 3.84 us -> 10.3 us  [the longest x1 5.31 us: local(): lax.all_to_all(split_heads(kv_pool, own), 'cp', split_axis=0, concat_axis...]
    unnamed x54 -> x58, local copies, waits for them, and re-layouts: 17.4 us -> 12.2 us
    ppermute x19, starting transfers between devices: 19 us -> 14.6 us  [swap(): return lax.ppermute(array, 'cp', [(i, i ^ bit) for i in range(count)])]
    pallas_call x2 -> x3, Pallas kernels: 8.86 us -> 4.66 us  [the longest x1 3.22 us: pack(): pl.pallas_call(pack_kernel, grid_spec=pltpu.PrefetchScalarGridSpec(num_sc...]
    dot_general x2, matrix products: 8.28 us -> 11.7 us  [local(): jnp.dot(attended, w_out[:, at:at + wide], preferred_element_type=jnp.floa...]
  transfers between devices with their start and end apart: 22 -> 25, of which waited for: 13 -> 11; matrix products, arithmetic and copies ran while one was open for 3% -> 13% of each run, Pallas kernels for 5% -> 6%
where the time goes in v3:
time: 189 us; the launch traced here: 187 us
  waiting for transfers between devices  51.4 us (27%)
  starting transfers between devices  42.7 us (23%)
  Pallas kernels  31 us (16%)
  local copies, waits for them, and re-layouts  22.8 us (12%)
  between operations  17.1 us (9%)
  matrix products  11.7 us (6%)
  other arithmetic  10.5 us (6%)
    ppermute x19, waiting for transfers between devices, swap(): return lax.ppermute(array, 'cp', [(i, i ^ bit) for i in range(count)])  26.4 us
    all_to_all x1, waiting for transfers between devices, local(): lax.all_to_all(split_heads(kv_pool, own), 'cp', split_axis=0, concat_axis...  20.5 us
    pallas_call x1, Pallas kernels, attention(): pl.pallas_call(functools.partial(attention_kernel, tile, ordered), grid_s...  15.8 us
    all_to_all x1, starting transfers between devices, local(): lax.all_to_all(blocks, ('req', 'cp'), split_axis=0, concat_axis=0, tiled=...  15.1 us
    ppermute x19, starting transfers between devices, swap(): return lax.ppermute(array, 'cp', [(i, i ^ bit) for i in range(count)])  14.6 us
    unnamed x58, local copies, waits for them, and re-layouts  12.2 us
    dot_general x2, matrix products, local(): jnp.dot(attended, w_out[:, at:at + wide], preferred_element_type=jnp.floa...  11.7 us
    pallas_call x1, Pallas kernels, query_project(): pl.pallas_call(query_kernel, grid_spec=pltpu.PrefetchScalarGridSpec(num_s...  10.5 us
  transfers between devices with their start and end apart: 25, of which 11 were waited for; matrix products, arithmetic and copies ran while one was open for 13% of the time, Pallas kernels for 6%

profile of v3, /device:TPU:0, one launch (start us, length us, event | category | flops | bytes accessed | tf_op | source)
XLA Modules:
  0.0 187.1 jit_solution(10468535707353651002)
XLA Ops:
  7.2 1.0 copy-done.5
  8.2 1.4 copy-done.8
  9.9 1.3 copy-done.2
  11.3 5.3 %all-to-all-start = ((bf16[8,32,16,256]{3,2,1,0:T(8,128)(2,1)}), bf16[8,32,16,256]{3,2,1,0:T(8,128)(2,1)S(1)}, u32[]{:S(2)}, u32[]{:S(2)}) async-start(bf16[8,32,16,256]{3,2,1,0:T(8,128)(2,1)} %copy-done.2), calls=%async_computation | async-start | bytes 4194304 | tf_op jit(solution)/shard_map/all_to_all | solution.py:443
  21.9 0.8 pad_maximum_fusion
  22.7 20.5 %all-to-all-done.pool_ref.mixed_ref.refs_0_ = bf16[8,32,16,256]{3,2,1,0:T(8,128)(2,1)S(1)} async-done(((bf16[8,32,16,256]{3,2,1,0:T(8,128)(2,1)}), bf16[8,32,16,256]{3,2,1,0:T(8,128)(2,1)S(1)}, u32[]{:S(2)}, u32[]{:S(2)}) %all-to-all-start) | async-done | bytes 2097184 | tf_op jit(solution)/shard_map/all_to_all | solution.py:443
  43.2 3.2 %shard_map.123 = (bf16[4,6,128,256]{3,2,1,0:T(8,128)(2,1)S(1)}, bf16[6,128,256]{2,1,0:T(8,128)(2,1)S(1)}, bf16[6,128,256]{2,1,0:T(8,128)(2,1)}, bf16[6,128,256]{2,1,0:T(8,128)(2,1)}) custom-call(s32[1]{0:T(128)} %bitcast.group_ref, s32[4,24]{1,0:T(4,128)S(1)} %copy-done.13, s32[4,24]{1,0:T(4,128)S(1)} %copy-done.14, ...), custom_call_target="tpu_custom_call" | custom-call | tf_op jit(solution)/shard_map/pallas_call | solution.py:112
  46.4 1.2 copy-done.7
  47.6 0.8 copy-done.15
  48.4 2.2 %copy-done.4 = bf16[1024,2048]{1,0:T(8,128)(2,1)S(1)} copy-done((bf16[1024,2048]{1,0:T(8,128)(2,1)S(1)}, bf16[1024,2048]{1,0:T(8,128)(2,1)}, u32[]{:S(2)}) %copy-start.4) | copy-done | bytes 4194328
  50.6 1.2 shard_map.125
  51.9 1.4 copy-done.3
  53.3 5.0 %all-to-all-start.1 = ((bf16[4,6,128,256]{3,2,1,0:T(8,128)(2,1)}), bf16[4,6,128,256]{3,2,1,0:T(8,128)(2,1)}, u32[]{:S(2)}, u32[]{:S(2)}) async-start(bf16[4,6,128,256]{3,2,1,0:T(8,128)(2,1)} %copy-done.7), calls=%async_computation.2 | async-start | bytes 3145728 | tf_op jit(solution)/shard_map/all_to_all | solution.py:452
  59.8 9.1 %collective-permute-done.27.refs_4_ = bf16[32,8192]{1,0:T(8,128)(2,1)S(1)} collective-permute-done((bf16[32,8192]{1,0:T(8,128)(2,1)S(1)}, bf16[32,8192]{1,0:T(8,128)(2,1)S(1)}, u32[]{:S(2)}, u32[]{:S(2)}) %collective-permute-start.27) | collective-permute-done | bytes 524320 | tf_op jit(solution)/shard_map/ppermute | solution.py:388
  69.6 3.5 %collective-permute-start.29 = (bf16[32,4096]{1,0:T(8,128)(2,1)}, bf16[32,4096]{1,0:T(8,128)(2,1)S(1)}, u32[]{:S(2)}, u32[]{:S(2)}) collective-permute-start(bf16[32,4096]{1,0:T(8,128)(2,1)} %slice.34), channel_id=1, source_target_pairs={{0,2},{1,3},{2,0},{3,1},{4,6},{5,7},{6,4},{7,5},{8,10},{9,11},{10,... | collective-permute-start | bytes 786440 | tf_op jit(solution)/shard_map/ppermute | solution.py:388
  73.1 1.7 slice.35
  76.4 0.8 copy-done.10
  77.2 1.7 collective-permute-start.33
  79.6 1.2 broadcast_in_dim.25
  80.9 2.9 %collective-permute-done.29.refs_6_ = bf16[32,4096]{1,0:T(8,128)(2,1)S(1)} collective-permute-done((bf16[32,4096]{1,0:T(8,128)(2,1)}, bf16[32,4096]{1,0:T(8,128)(2,1)S(1)}, u32[]{:S(2)}, u32[]{:S(2)}) %collective-permute-start.29) | collective-permute-done | bytes 262176 | tf_op jit(solution)/shard_map/ppermute | solution.py:388
  83.8 3.9 %collective-permute-done.31.refs_8_ = bf16[32,4096]{1,0:T(8,128)(2,1)} collective-permute-done((bf16[32,4096]{1,0:T(8,128)(2,1)}, bf16[32,4096]{1,0:T(8,128)(2,1)}, u32[]{:S(2)}, u32[]{:S(2)}) %collective-permute-start.31) | collective-permute-done | bytes 262176 | tf_op jit(solution)/shard_map/ppermute | solution.py:388
  89.6 1.0 copy-done.11
  90.6 10.5 %shard_map.124.q_ref = f32[256,1024]{1,0:T(8,128)} custom-call(s32[1]{0:T(128)} %bitcast.3.rank_ref, bf16[32,8192]{1,0:T(8,128)(2,1)S(1)} %bitcast.93, bf16[32,8192]{1,0:T(8,128)(2,1)S(1)} %copy-done.11, bf16[32,8192]{1,0:T(8,128)(2,1)} %collective-permute-done.25.refs_2_, bf16[32,8192]{1,0:T(8,128)(2,1)} %collective-permute-done.26.refs_3_, ...), custom_call_target="tpu_custom_call" | custom-call | flops 1024 | bytes 1024 | tf_op jit(solution)/shard_map/pallas_call | solution.py:360
  101.2 1.6 conditional.1
  101.2 0.8 collective-permute-start.10
  102.8 0.9 copy-done.16
  103.8 15.8 %shard_map.126 = (bf16[256,1024]{1,0:T(8,128)(2,1)S(1)}, bf16[256,256]{1,0:T(8,128)(2,1)S(1)}) custom-call(s32[4]{0:T(128)S(1)} %copy-done.17, s32[1]{0:T(128)} %bitcast.group_ref, s32[4,24]{1,0:T(4,128)S(1)} %copy-done.13, s32[4,24]{1,0:T(4,128)S(1)} %copy-done.14, f32[256,1024]{1,0:T(8,128)S(1)} %copy-done.9, f32[256,128]{1,0:T(8,128)S(1)} %get-tuple-element.127.cos_ref, ...), custom_call_target="tpu_custom_call" | custom-call | flops 3489660928 | bytes 1572864 | tf_op jit(solution)/shard_map/pallas_call | solution.py:234
  119.6 5.9 %fusion.4 = bf16[256,4096]{1,0:T(8,128)(2,1)S(1)} fusion(bf16[256,1024]{1,0:T(8,128)(2,1)S(1)} %get-tuple-element.137, bf16[1024,8192]{1,0:T(8,128)(2,1)} %param.31), kind=kOutput, calls=%fused_computation.5 | convolution fusion | flops 2148532224 | bytes 11010048 | tf_op jit(solution)/shard_map/dot_general | solution.py:497
  125.6 1.1 dynamic-slice_bitcast_fusion.1
  127.5 0.8 bitcast_select_fusion
  128.3 15.1 %all-to-all-start.2 = ((bf16[32,16,256]{2,1,0:T(8,128)(2,1)}), bf16[32,16,256]{2,1,0:T(8,128)(2,1)S(1)}, u32[]{:S(2)}, u32[]{:S(2)}) async-start(bf16[32,16,256]{2,1,0:T(8,128)(2,1)} %bitcast_select_fusion), calls=%async_computation.3 | async-start | bytes 524288 | tf_op jit(solution)/shard_map/all_to_all | solution.py:529
  143.4 5.7 %fusion.7 = bf16[256,4096]{1,0:T(8,128)(2,1)S(1)} fusion(bf16[256,1024]{1,0:T(8,128)(2,1)S(1)} %copy-done.19, bf16[1024,8192]{1,0:T(8,128)(2,1)} %param.31), kind=kOutput, calls=%fused_computation.6 | convolution fusion | flops 2148532224 | bytes 11010048 | tf_op jit(solution)/shard_map/dot_general | solution.py:497
  149.6 4.4 %all-to-all-done.2 = bf16[32,16,256]{2,1,0:T(8,128)(2,1)S(1)} async-done(((bf16[32,16,256]{2,1,0:T(8,128)(2,1)}), bf16[32,16,256]{2,1,0:T(8,128)(2,1)S(1)}, u32[]{:S(2)}, u32[]{:S(2)}) %all-to-all-start.2) | async-done | bytes 262176 | tf_op jit(solution)/shard_map/all_to_all | solution.py:529
  154.0 0.8 reshape.260
  154.8 1.1 copy.23
  155.9 0.8 reshape.261
  156.8 1.8 fusion.11
  159.0 1.6 collective-permute-start.37
  160.6 1.5 fusion.10
  162.2 1.2 collective-permute-start.40
  163.4 1.2 collective-permute-start.42
  164.7 3.3 %collective-permute-done.35 = bf16[2,32,2048]{2,1,0:T(8,128)(2,1)S(1)} collective-permute-done((bf16[2,32,2048]{2,1,0:T(8,128)(2,1)S(1)}, bf16[2,32,2048]{2,1,0:T(8,128)(2,1)S(1)}, u32[]{:S(2)}, u32[]{:S(2)}) %collective-permute-start.35) | collective-permute-done | bytes 262176 | tf_op jit(solution)/shard_map/ppermute | solution.py:388
  168.8 1.4 collective-permute-start.38
  170.2 3.3 %collective-permute-done.40 = bf16[2,32,2048]{2,1,0:T(8,128)(2,1)S(1)} collective-permute-done((bf16[2,32,2048]{2,1,0:T(8,128)(2,1)S(1)}, bf16[2,32,2048]{2,1,0:T(8,128)(2,1)S(1)}, u32[]{:S(2)}, u32[]{:S(2)}) %collective-permute-start.40) | collective-permute-done | bytes 262176 | tf_op jit(solution)/shard_map/ppermute | solution.py:388
  174.3 1.5 collective-permute-start.43
  175.8 0.8 collective-permute-done.36
  176.7 2.1 %collective-permute-done.41 = bf16[32,2048]{1,0:T(8,128)(2,1)S(1)} collective-permute-done((bf16[32,2048]{1,0:T(8,128)(2,1)S(1)}, bf16[32,2048]{1,0:T(8,128)(2,1)S(1)}, u32[]{:S(2)}, u32[]{:S(2)}) %collective-permute-start.41) | collective-permute-done | bytes 131104 | tf_op jit(solution)/shard_map/ppermute | solution.py:388
  179.4 0.9 fusion.12
  (118 shorter events, 14.3 us)
Async XLA Ops:
  7.2 52.3 %copy-start = (s32[4,2]{0,1:T(2,128)S(1)}, s32[4,2]{0,1:T(2,128)}, u32[]{:S(2)}) copy-start(s32[4,2]{0,1:T(2,128)} %param.36) | copy-start | bytes 100
  8.2 1.4 copy-start.8
  9.8 1.4 copy-start.2
  11.2 5.4 %copy-start.17 = (s32[4]{0:T(128)S(1)}, s32[4]{0:T(128)}, u32[]{:S(2)}) copy-start(s32[4]{0:T(128)} %length_ref.1) | copy-start | bytes 52
  11.2 6.1 %copy-start.13 = (s32[4,24]{1,0:T(4,128)S(1)}, s32[4,24]{1,0:T(4,128)}, u32[]{:S(2)}) copy-start(s32[4,24]{1,0:T(4,128)} %holder_ref.3) | copy-start | bytes 1156
  11.2 6.2 %copy-start.25 = (pred[4,4]{1,0:T(4,128)(4,1)S(1)}, pred[4,4]{1,0:T(4,128)(4,1)}, u32[]{:S(2)}) copy-start(pred[4,4]{1,0:T(4,128)(4,1)} %constant.152) | copy-start | bytes 52
  11.2 6.2 %copy-start.26 = (pred[4,4]{1,0:T(4,128)(4,1)S(1)}, pred[4,4]{1,0:T(4,128)(4,1)}, u32[]{:S(2)}) copy-start(pred[4,4]{1,0:T(4,128)(4,1)} %constant.153) | copy-start | bytes 52
  11.2 6.3 %copy-start.27 = (pred[4,4]{1,0:T(4,128)(4,1)S(1)}, pred[4,4]{1,0:T(4,128)(4,1)}, u32[]{:S(2)}) copy-start(pred[4,4]{1,0:T(4,128)(4,1)} %constant.154) | copy-start | bytes 52
  11.2 6.3 %copy-start.28 = (pred[4,4]{1,0:T(4,128)(4,1)S(1)}, pred[4,4]{1,0:T(4,128)(4,1)}, u32[]{:S(2)}) copy-start(pred[4,4]{1,0:T(4,128)(4,1)} %constant.155) | copy-start | bytes 52
  11.2 32.0 %copy-start.14 = (s32[4,24]{1,0:T(4,128)S(1)}, s32[4,24]{1,0:T(4,128)}, u32[]{:S(2)}) copy-start(s32[4,24]{1,0:T(4,128)} %slot_ref.3) | copy-start | bytes 1156
  11.3 32.0 %all-to-all-start = ((bf16[8,32,16,256]{3,2,1,0:T(8,128)(2,1)}), bf16[8,32,16,256]{3,2,1,0:T(8,128)(2,1)S(1)}, u32[]{:S(2)}, u32[]{:S(2)}) async-start(bf16[8,32,16,256]{3,2,1,0:T(8,128)(2,1)} %copy-done.2), calls=%async_computation | async-start | bytes 4194304 | tf_op jit(solution)/shard_map/all_to_all | solution.py:443
  16.6 86.2 %reduce-scatter.2.cloned.1.call-start = ((), (), s32[]{:S(2)}) async-start(), calls=%async_computation.4 | async-start | bytes 2359296 | tf_op jit(solution)/shard_map/reduce_scatter | solution.py:455
  48.4 2.2 %copy-start.4 = (bf16[1024,2048]{1,0:T(8,128)(2,1)S(1)}, bf16[1024,2048]{1,0:T(8,128)(2,1)}, u32[]{:S(2)}) copy-start(bf16[1024,2048]{1,0:T(8,128)(2,1)} %weight_ref.1) | copy-start | bytes 12582916
  51.9 1.4 copy-start.3
  53.2 5.0 %copy-start.6 = (bf16[1,32,8192]{2,1,0:T(8,128)(2,1)S(1)}, bf16[1,32,8192]{2,1,0:T(8,128)(2,1)}, u32[]{:S(2)}) copy-start(bf16[1,32,8192]{2,1,0:T(8,128)(2,1)} %param.27) | copy-start | bytes 1572868
  53.3 49.5 %all-to-all-start.1 = ((bf16[4,6,128,256]{3,2,1,0:T(8,128)(2,1)}), bf16[4,6,128,256]{3,2,1,0:T(8,128)(2,1)}, u32[]{:S(2)}, u32[]{:S(2)}) async-start(bf16[4,6,128,256]{3,2,1,0:T(8,128)(2,1)} %copy-done.7), calls=%async_computation.2 | async-start | bytes 3145728 | tf_op jit(solution)/shard_map/all_to_all | solution.py:452
  58.3 10.6 %collective-permute-start.27 = (bf16[32,8192]{1,0:T(8,128)(2,1)S(1)}, bf16[32,8192]{1,0:T(8,128)(2,1)S(1)}, u32[]{:S(2)}, u32[]{:S(2)}) collective-permute-start(bf16[32,8192]{1,0:T(8,128)(2,1)S(1)} %bitcast.90), channel_id=1, source_target_pairs={{0,4},{1,5},{2,6},{3,7},{4,0},{5,1},{6,2},{7,3},{8,12},{9,13},{10,... | collective-permute-start | bytes 1572872 | tf_op jit(solution)/shard_map/ppermute | solution.py:388
  58.8 14.3 %collective-permute-start.25 = (bf16[32,8192]{1,0:T(8,128)(2,1)S(1)}, bf16[32,8192]{1,0:T(8,128)(2,1)}, u32[]{:S(2)}, u32[]{:S(2)}) collective-permute-start(bf16[32,8192]{1,0:T(8,128)(2,1)S(1)} %bitcast.91), channel_id=1, source_target_pairs={{0,2},{1,3},{2,0},{3,1},{4,6},{5,7},{6,4},{7,5},{8,10},{9,11},{10,... | collective-permute-start | bytes 1572872 | tf_op jit(solution)/shard_map/ppermute | solution.py:388
  59.4 16.9 %collective-permute-start.24 = (bf16[32,8192]{1,0:T(8,128)(2,1)S(1)}, bf16[32,8192]{1,0:T(8,128)(2,1)S(1)}, u32[]{:S(2)}, u32[]{:S(2)}) collective-permute-start(bf16[32,8192]{1,0:T(8,128)(2,1)S(1)} %bitcast.92), channel_id=1, source_target_pairs={{0,1},{1,0},{2,3},{3,2},{4,5},{5,4},{6,7},{7,6},{8,9},{9,8},{10,11... | collective-permute-start | bytes 1572872 | tf_op jit(solution)/shard_map/ppermute | solution.py:388
  69.6 14.2 %collective-permute-start.29 = (bf16[32,4096]{1,0:T(8,128)(2,1)}, bf16[32,4096]{1,0:T(8,128)(2,1)S(1)}, u32[]{:S(2)}, u32[]{:S(2)}) collective-permute-start(bf16[32,4096]{1,0:T(8,128)(2,1)} %slice.34), channel_id=1, source_target_pairs={{0,2},{1,3},{2,0},{3,1},{4,6},{5,7},{6,4},{7,5},{8,10},{9,11},{10,... | collective-permute-start | bytes 786440 | tf_op jit(solution)/shard_map/ppermute | solution.py:388
  74.8 12.9 %collective-permute-start.31 = (bf16[32,4096]{1,0:T(8,128)(2,1)}, bf16[32,4096]{1,0:T(8,128)(2,1)}, u32[]{:S(2)}, u32[]{:S(2)}) collective-permute-start(bf16[32,4096]{1,0:T(8,128)(2,1)} %slice.35), channel_id=1, source_target_pairs={{0,4},{1,5},{2,6},{3,7},{4,0},{5,1},{6,2},{7,3},{8,12},{9,13},{10,... | collective-permute-start | bytes 786440 | tf_op jit(solution)/shard_map/ppermute | solution.py:388
  75.2 14.4 %collective-permute-start.26 = (bf16[32,8192]{1,0:T(8,128)(2,1)}, bf16[32,8192]{1,0:T(8,128)(2,1)}, u32[]{:S(2)}, u32[]{:S(2)}) collective-permute-start(bf16[32,8192]{1,0:T(8,128)(2,1)} %collective-permute-done.25.refs_2_), channel_id=1, source_target_pairs={{0,1},{1,0},{2,3},{3,2},{4,5},{5,4},{6,7},{7,6},{8,9},{9,8},{10,11... | collective-permute-start | bytes 1572872 | tf_op jit(solution)/shard_map/ppermute | solution.py:388
  75.2 14.4 %collective-permute-start.28 = (bf16[32,8192]{1,0:T(8,128)(2,1)S(1)}, bf16[32,8192]{1,0:T(8,128)(2,1)}, u32[]{:S(2)}, u32[]{:S(2)}) collective-permute-start(bf16[32,8192]{1,0:T(8,128)(2,1)S(1)} %collective-permute-done.27.refs_4_), channel_id=1, source_target_pairs={{0,1},{1,0},{2,3},{3,2},{4,5},{5,4},{6,7},{7,6},{8,9},{9,8},{10,11... | collective-permute-start | bytes 1572872 | tf_op jit(solution)/shard_map/ppermute | solution.py:388
  77.2 25.6 %collective-permute-start.33 = (bf16[6,128,256]{2,1,0:T(8,128)(2,1)}, bf16[6,128,256]{2,1,0:T(8,128)(2,1)}, u32[]{:S(2)}, u32[]{:S(2)}) collective-permute-start(bf16[6,128,256]{2,1,0:T(8,128)(2,1)} %copy-done.15), channel_id=1, source_target_pairs={{0,8},{8,0},{16,24},{24,16},{1,9},{9,1},{17,25},{25,17},{2,10},{10... | collective-permute-start | bytes 1179656 | tf_op jit(solution)/shard_map/ppermute | solution.py:453
  83.8 5.2 %collective-permute-start.30 = (bf16[32,4096]{1,0:T(8,128)(2,1)S(1)}, bf16[32,4096]{1,0:T(8,128)(2,1)}, u32[]{:S(2)}, u32[]{:S(2)}) collective-permute-start(bf16[32,4096]{1,0:T(8,128)(2,1)S(1)} %collective-permute-done.29.refs_6_), channel_id=1, source_target_pairs={{0,1},{1,0},{2,3},{3,2},{4,5},{5,4},{6,7},{7,6},{8,9},{9,8},{10,11... | collective-permute-start | bytes 786440 | tf_op jit(solution)/shard_map/ppermute | solution.py:388
  87.7 1.9 %collective-permute-start.32 = (bf16[32,4096]{1,0:T(8,128)(2,1)}, bf16[32,4096]{1,0:T(8,128)(2,1)}, u32[]{:S(2)}, u32[]{:S(2)}) collective-permute-start(bf16[32,4096]{1,0:T(8,128)(2,1)} %collective-permute-done.31.refs_8_), channel_id=1, source_target_pairs={{0,1},{1,0},{2,3},{3,2},{4,5},{5,4},{6,7},{7,6},{8,9},{9,8},{10,11... | collective-permute-start | bytes 786440 | tf_op jit(solution)/shard_map/ppermute | solution.py:388
  101.2 1.7 copy-start.9
  101.2 1.7 copy-start.12
  101.2 0.8 collective-permute-start.10
  119.6 6.0 %copy-start.18 = (bf16[256,1024]{1,0:T(8,128)(2,1)}, bf16[256,1024]{1,0:T(8,128)(2,1)S(1)}, u32[]{:S(2)}) copy-start(bf16[256,1024]{1,0:T(8,128)(2,1)S(1)} %get-tuple-element.137) | copy-start | bytes 1572868
  125.5 2.8 %copy-start.22 = (bf16[256,4096]{1,0:T(8,128)(2,1)}, bf16[256,4096]{1,0:T(8,128)(2,1)S(1)}, u32[]{:S(2)}) copy-start(bf16[256,4096]{1,0:T(8,128)(2,1)S(1)} %fusion.4) | copy-start | bytes 6291460
  125.5 1.9 %copy-start.24 = (pred[32]{0:T(512)(128)(4,1)S(1)}, pred[32]{0:T(512)(128)(4,1)}, u32[]{:S(2)}) copy-start(pred[32]{0:T(512)(128)(4,1)} %broadcast_in_dim.25) | copy-start | bytes 100
  125.6 17.9 %copy-start.19 = (bf16[256,1024]{1,0:T(8,128)(2,1)S(1)}, bf16[256,1024]{1,0:T(8,128)(2,1)}, u32[]{:S(2)}) copy-start(bf16[256,1024]{1,0:T(8,128)(2,1)} %copy-done.18) | copy-start | bytes 1572868
  126.6 30.1 %collective-permute-start.34 = (bf16[2,2,32,4096]{3,2,1,0:T(8,128)(2,1)}, bf16[2,2,32,4096]{3,2,1,0:T(8,128)(2,1)}, u32[]{:S(2)}, u32[]{:S(2)}) collective-permute-start(bf16[2,2,32,4096]{3,2,1,0:T(8,128)(2,1)} %dynamic-slice_bitcast_fusion.1), channel_id=1, source_target_pairs={{0,1},{1,0},{2,3},{3,2},{4,5},{5,4},{6,7},{7,6},{8,9},{9,8},{10,11... | collective-permute-start | bytes 3145736 | tf_op jit(solution)/shard_map/ppermute | solution.py:388
  128.3 25.7 %all-to-all-start.2 = ((bf16[32,16,256]{2,1,0:T(8,128)(2,1)}), bf16[32,16,256]{2,1,0:T(8,128)(2,1)S(1)}, u32[]{:S(2)}, u32[]{:S(2)}) async-start(bf16[32,16,256]{2,1,0:T(8,128)(2,1)} %bitcast_select_fusion), calls=%async_computation.3 | async-start | bytes 524288 | tf_op jit(solution)/shard_map/all_to_all | solution.py:529
  149.2 7.5 %copy-start.20 = (bf16[256,4096]{1,0:T(8,128)(2,1)}, bf16[256,4096]{1,0:T(8,128)(2,1)S(1)}, u32[]{:S(2)}) copy-start(bf16[256,4096]{1,0:T(8,128)(2,1)S(1)} %fusion.7) | copy-start | bytes 6291460
  149.3 11.3 %collective-permute-start.39 = (bf16[2,2,32,4096]{3,2,1,0:T(8,128)(2,1)S(1)}, bf16[2,2,32,4096]{3,2,1,0:T(8,128)(2,1)}, u32[]{:S(2)}, u32[]{:S(2)}) collective-permute-start(bf16[2,2,32,4096]{3,2,1,0:T(8,128)(2,1)S(1)} %dynamic-slice_bitcast_fusion), channel_id=1, source_target_pairs={{0,1},{1,0},{2,3},{3,2},{4,5},{5,4},{6,7},{7,6},{8,9},{9,8},{10,11... | collective-permute-start | bytes 3145736 | tf_op jit(solution)/shard_map/ppermute | solution.py:388
  158.5 2.0 %copy-start.21 = (bf16[256,4096]{1,0:T(8,128)(2,1)S(1)}, bf16[256,4096]{1,0:T(8,128)(2,1)}, u32[]{:S(2)}) copy-start(bf16[256,4096]{1,0:T(8,128)(2,1)} %copy-done.20) | copy-start | bytes 6291460
  158.7 9.2 %collective-permute-start.35 = (bf16[2,32,2048]{2,1,0:T(8,128)(2,1)S(1)}, bf16[2,32,2048]{2,1,0:T(8,128)(2,1)S(1)}, u32[]{:S(2)}, u32[]{:S(2)}) collective-permute-start(bf16[2,32,2048]{2,1,0:T(8,128)(2,1)S(1)} %dynamic-slice_bitcast_fusion.5), channel_id=1, source_target_pairs={{0,2},{1,3},{2,0},{3,1},{4,6},{5,7},{6,4},{7,5},{8,10},{9,11},{10,... | collective-permute-start | bytes 786440 | tf_op jit(solution)/shard_map/ppermute | solution.py:388
  159.0 9.7 %collective-permute-start.37 = (bf16[2,32,2048]{2,1,0:T(8,128)(2,1)S(1)}, bf16[2,32,2048]{2,1,0:T(8,128)(2,1)S(1)}, u32[]{:S(2)}, u32[]{:S(2)}) collective-permute-start(bf16[2,32,2048]{2,1,0:T(8,128)(2,1)S(1)} %dynamic-slice_bitcast_fusion.4), channel_id=1, source_target_pairs={{0,4},{1,5},{2,6},{3,7},{4,0},{5,1},{6,2},{7,3},{8,12},{9,13},{10,... | collective-permute-start | bytes 786440 | tf_op jit(solution)/shard_map/ppermute | solution.py:388
  162.2 11.4 %collective-permute-start.40 = (bf16[2,32,2048]{2,1,0:T(8,128)(2,1)S(1)}, bf16[2,32,2048]{2,1,0:T(8,128)(2,1)S(1)}, u32[]{:S(2)}, u32[]{:S(2)}) collective-permute-start(bf16[2,32,2048]{2,1,0:T(8,128)(2,1)S(1)} %dynamic-slice_bitcast_fusion.3), channel_id=1, source_target_pairs={{0,2},{1,3},{2,0},{3,1},{4,6},{5,7},{6,4},{7,5},{8,10},{9,11},{10,... | collective-permute-start | bytes 786440 | tf_op jit(solution)/shard_map/ppermute | solution.py:388
  163.4 10.8 %collective-permute-start.42 = (bf16[2,32,2048]{2,1,0:T(8,128)(2,1)S(1)}, bf16[2,32,2048]{2,1,0:T(8,128)(2,1)S(1)}, u32[]{:S(2)}, u32[]{:S(2)}) collective-permute-start(bf16[2,32,2048]{2,1,0:T(8,128)(2,1)S(1)} %dynamic-slice_bitcast_fusion.2), channel_id=1, source_target_pairs={{0,4},{1,5},{2,6},{3,7},{4,0},{5,1},{6,2},{7,3},{8,12},{9,13},{10,... | collective-permute-start | bytes 786440 | tf_op jit(solution)/shard_map/ppermute | solution.py:388
  168.0 8.6 %collective-permute-start.36 = (bf16[32,2048]{1,0:T(8,128)(2,1)S(1)}, bf16[32,2048]{1,0:T(8,128)(2,1)S(1)}, u32[]{:S(2)}, u32[]{:S(2)}) collective-permute-start(bf16[32,2048]{1,0:T(8,128)(2,1)S(1)} %fusion.17), channel_id=1, source_target_pairs={{0,4},{1,5},{2,6},{3,7},{4,0},{5,1},{6,2},{7,3},{8,12},{9,13},{10,... | collective-permute-start | bytes 393224 | tf_op jit(solution)/shard_map/ppermute | solution.py:388
  168.8 7.8 %collective-permute-start.38 = (bf16[32,2048]{1,0:T(8,128)(2,1)S(1)}, bf16[32,2048]{1,0:T(8,128)(2,1)S(1)}, u32[]{:S(2)}, u32[]{:S(2)}) collective-permute-start(bf16[32,2048]{1,0:T(8,128)(2,1)S(1)} %fusion.18), channel_id=1, source_target_pairs={{0,2},{1,3},{2,0},{3,1},{4,6},{5,7},{6,4},{7,5},{8,10},{9,11},{10,... | collective-permute-start | bytes 393224 | tf_op jit(solution)/shard_map/ppermute | solution.py:388
  173.6 5.8 %copy-start.23 = (bf16[1,32,8192]{2,1,0:T(8,128)(2,1)S(1)}, bf16[1,32,8192]{2,1,0:T(8,128)(2,1)}, u32[]{:S(2)}) copy-start(bf16[1,32,8192]{2,1,0:T(8,128)(2,1)} %param.28) | copy-start | bytes 1572868
  173.6 5.2 %collective-permute-start.41 = (bf16[32,2048]{1,0:T(8,128)(2,1)S(1)}, bf16[32,2048]{1,0:T(8,128)(2,1)S(1)}, u32[]{:S(2)}, u32[]{:S(2)}) collective-permute-start(bf16[32,2048]{1,0:T(8,128)(2,1)S(1)} %fusion.19), channel_id=1, source_target_pairs={{0,4},{1,5},{2,6},{3,7},{4,0},{5,1},{6,2},{7,3},{8,12},{9,13},{10,... | collective-permute-start | bytes 393224 | tf_op jit(solution)/shard_map/ppermute | solution.py:388
  174.3 5.0 %collective-permute-start.43 = (bf16[32,2048]{1,0:T(8,128)(2,1)S(1)}, bf16[32,2048]{1,0:T(8,128)(2,1)S(1)}, u32[]{:S(2)}, u32[]{:S(2)}) collective-permute-start(bf16[32,2048]{1,0:T(8,128)(2,1)S(1)} %fusion.20), channel_id=1, source_target_pairs={{0,2},{1,3},{2,0},{3,1},{4,6},{5,7},{6,4},{7,5},{8,10},{9,11},{10,... | collective-permute-start | bytes 393224 | tf_op jit(solution)/shard_map/ppermute | solution.py:388
  176.6 3.7 %copy-start.1 = (s32[4,2]{0,1:T(2,128)S(1)}, s32[4,2]{0,1:T(2,128)}, u32[]{:S(2)}) copy-start(s32[4,2]{0,1:T(2,128)} %param.36) | copy-start | bytes 100
  (6 other events, 5.8 us)
Sparse Core Ops, SparseCore 0:
  53.4 45.2 reduce-scatter.1
